TPU v7x, 256 devices: a whole 4x4x8 slice. The times are simulated.
256 devices in a mesh: dp: 8 (over z), ctx: 32 (over y, x, core).
Axes of the slice: x: 4, y: 4, z: 8, core: 2. Of those that a mesh axis runs over, the one named last changes fastest.
Arguments:
- queries: bfloat16 [8, 4096, 16, 128], P('dp', 'ctx'), may hold values from -6 to 6
- key_rows: bfloat16 [8, 4096, 16, 128], P('dp', 'ctx'), may hold values from -6 to 6
- value_rows: bfloat16 [8, 4096, 16, 128], P('dp', 'ctx'), may hold values from -6 to 6
- attn_out: bfloat16 [8, 4096, 16, 128], P('dp', 'ctx'), may hold values from -6 to 6
- out_grad: bfloat16 [8, 4096, 16, 128], P('dp', 'ctx'), may hold values from -6 to 6
- log_sums: float32 [8, 16, 4096], P('dp', None, 'ctx'), may hold values from 5 to 7
- chosen: int32 [8, 32, 16, 3], P('dp', 'ctx'), may hold values from 0 to 31, as said below
- inputs: bfloat16 [8, 4096, 2048], P('dp', 'ctx'), may hold values from -6 to 6
Outputs:
- query_grad: bfloat16 [8, 4096, 16, 128], P('dp', 'ctx')
- key_grad: bfloat16 [8, 4096, 16, 128], P('dp', 'ctx')
- value_grad: bfloat16 [8, 4096, 16, 128], P('dp', 'ctx')
- weight_grad: float32 [2048, 2048], P(('dp', 'ctx'))
Inputs may be any that keep to these rules, and one draw needn't show every extreme that they name: `chosen`: within one query block and head the entries name different key blocks; each entry is at most the query block's own index i, and is below i for at most min(3, i) of each head's entries. No key block is named by more than 2 heads of one query block.
All inputs are finite; a program needn't handle non-finite values.
Results may differ from a plain program's by a relative error of at most 0.006.
Values may be sent and summed in bfloat16 or wider, within the bound.
A program may use at most 128 MiB of HBM per device.

v0:
```python
import jax
import jax.numpy as jnp
from jax import lax
from jax.sharding import PartitionSpec as P

CAP = 2


slot_group = 8


def slot_routes(chosen_all, block_count, head_count, width):
    entries = head_count * width
    flat = chosen_all.reshape(block_count, entries)
    source = jnp.arange(block_count, dtype=jnp.int32)[:, None]
    live = flat < source
    order = jnp.arange(entries, dtype=jnp.int32)
    earlier = (
        (flat[:, :, None] == flat[:, None, :])
        & live[:, None, :]
        & (order[None, None, :] < order[None, :, None])
    )
    ranks = jnp.sum(earlier.astype(jnp.int32), -1)
    block_ids = jnp.arange(block_count, dtype=jnp.int32)
    slot_ids = jnp.arange(CAP, dtype=jnp.int32)
    routes = (
        live[:, :, None, None]
        & (flat[:, :, None, None] == block_ids[None, None, :, None])
        & (ranks[:, :, None, None] == slot_ids[None, None, None, :])
    )
    owners = order // width
    head_table = (owners[:, None] == jnp.arange(head_count, dtype=jnp.int32)[None, :]).astype(
        jnp.int32
    )
    return jnp.einsum("sedc,eh->sdch", routes.astype(jnp.int32), head_table)


def per_device(queries, key_rows, value_rows, attn_out, out_grad, log_sums, chosen, inputs):
    query_local = queries[0]
    key_local = key_rows[0]
    value_local = value_rows[0]
    grad_local = out_grad[0]
    lse_local = log_sums[0]
    row_count, head_count, head_dim = query_local.shape
    softmax_scale = head_dim ** (-0.5)
    block_count = lax.axis_size("ctx")
    my_block = lax.axis_index("ctx")
    slot_count = block_count * CAP
    chosen_all = lax.all_gather(chosen, "ctx", axis=1, tiled=True)[0]
    route_all = slot_routes(chosen_all, block_count, head_count, chosen.shape[3])
    head_ids = jnp.arange(head_count, dtype=jnp.int32)
    send_map = lax.dynamic_index_in_dim(route_all, my_block, 0, keepdims=False).reshape(
        slot_count, head_count
    )
    recv_map = lax.dynamic_index_in_dim(route_all, my_block, 1, keepdims=False).reshape(
        slot_count, head_count
    )
    send_heads = jnp.sum(send_map * head_ids[None, :], -1)
    recv_heads = jnp.sum(recv_map * head_ids[None, :], -1)
    recv_onehot = recv_map.astype(jnp.float32)
    recv_live = jnp.sum(recv_onehot, -1)
    delta_local = jnp.sum(grad_local.astype(jnp.float32) * attn_out[0].astype(jnp.float32), -1).T
    query_slots = jnp.take(query_local, send_heads, axis=1).reshape(
        row_count, block_count, CAP, head_dim
    )
    grad_slots = jnp.take(grad_local, send_heads, axis=1).reshape(
        row_count, block_count, CAP, head_dim
    )
    lse_slots = jnp.take(lse_local, send_heads, axis=0).reshape(block_count, CAP, row_count)
    delta_slots = jnp.take(delta_local, send_heads, axis=0).reshape(block_count, CAP, row_count)
    query_recv, grad_recv = (
        lax.all_to_all(query_slots, "ctx", split_axis=1, concat_axis=1, tiled=True),
        lax.all_to_all(grad_slots, "ctx", split_axis=1, concat_axis=1, tiled=True),
    )
    stats_recv = lax.all_to_all(
        jnp.stack([lse_slots, delta_slots]), "ctx", split_axis=1, concat_axis=1, tiled=True
    )
    lse_recv = stats_recv[0].reshape(slot_count, row_count)
    delta_recv = stats_recv[1].reshape(slot_count, row_count)
    query_recv = query_recv.reshape(row_count, slot_count, head_dim)
    grad_recv = grad_recv.reshape(row_count, slot_count, head_dim)
    positions = jnp.arange(row_count, dtype=jnp.int32)
    causal = positions[:, None] >= positions[None, :]
    own_scores = (
        jnp.einsum("qhd,khd->hqk", query_local, key_local, preferred_element_type=jnp.float32)
        * softmax_scale
    )
    own_probs = jnp.where(causal[None], jnp.exp(own_scores - lse_local[:, :, None]), 0.0)
    own_low = own_probs.astype(jnp.bfloat16)
    own_dprobs = jnp.einsum(
        "qhd,khd->hqk", grad_local, value_local, preferred_element_type=jnp.float32
    )
    own_dscores = (own_probs * (own_dprobs - delta_local[:, :, None])).astype(jnp.bfloat16)
    query_own = softmax_scale * jnp.einsum(
        "hqk,khd->qhd", own_dscores, key_local, preferred_element_type=jnp.float32
    )
    key_own = softmax_scale * jnp.einsum(
        "hqk,qhd->khd", own_dscores, query_local, preferred_element_type=jnp.float32
    )
    value_own = jnp.einsum("hqk,qhd->khd", own_low, grad_local, preferred_element_type=jnp.float32)

    def group_pass(turn_index, totals):
        key_total, value_total, parts = totals
        first_slot = turn_index * slot_group
        query_group = lax.dynamic_slice_in_dim(query_recv, first_slot, slot_group, 1)
        grad_group = lax.dynamic_slice_in_dim(grad_recv, first_slot, slot_group, 1)
        head_group = lax.dynamic_slice_in_dim(recv_heads, first_slot, slot_group, 0)
        onehot_group = lax.dynamic_slice_in_dim(recv_onehot, first_slot, slot_group, 0)
        live_group = lax.dynamic_slice_in_dim(recv_live, first_slot, slot_group, 0)
        lse_group = lax.dynamic_slice_in_dim(lse_recv, first_slot, slot_group, 0)
        delta_group = lax.dynamic_slice_in_dim(delta_recv, first_slot, slot_group, 0)
        key_group = jnp.take(key_local, head_group, axis=1)
        value_group = jnp.take(value_local, head_group, axis=1)
        scores = (
            jnp.einsum("qgd,kgd->gqk", query_group, key_group, preferred_element_type=jnp.float32)
            * softmax_scale
        )
        probs = jnp.exp(scores - lse_group[:, :, None]) * live_group[:, None, None]
        probs_low = probs.astype(jnp.bfloat16)
        dprobs = jnp.einsum(
            "qgd,kgd->gqk", grad_group, value_group, preferred_element_type=jnp.float32
        )
        dscores = (probs * (dprobs - delta_group[:, :, None])).astype(jnp.bfloat16)
        query_part = (
            softmax_scale
            * jnp.einsum("gqk,kgd->qgd", dscores, key_group, preferred_element_type=jnp.float32)
        ).astype(jnp.bfloat16)
        key_part = softmax_scale * jnp.einsum(
            "gqk,qgd->kgd", dscores, query_group, preferred_element_type=jnp.float32
        )
        value_part = jnp.einsum(
            "gqk,qgd->kgd", probs_low, grad_group, preferred_element_type=jnp.float32
        )
        key_total = key_total + jnp.einsum(
            "kgd,gh->khd", key_part, onehot_group, precision=lax.Precision.HIGHEST
        )
        value_total = value_total + jnp.einsum(
            "kgd,gh->khd", value_part, onehot_group, precision=lax.Precision.HIGHEST
        )
        parts = lax.dynamic_update_slice_in_dim(parts, query_part, first_slot, 1)
        return (key_total, value_total, parts)

    zero_state = jnp.zeros((row_count, head_count, head_dim), jnp.float32)
    empty_parts = jnp.zeros((row_count, slot_count, head_dim), jnp.bfloat16)
    key_total, value_total, parts = lax.fori_loop(
        0, slot_count // slot_group, group_pass, (zero_state, zero_state, empty_parts)
    )
    returned = lax.all_to_all(
        parts.reshape(row_count, block_count, CAP, head_dim),
        "ctx",
        split_axis=1,
        concat_axis=1,
        tiled=True,
    )
    returned = returned.reshape(row_count, slot_count, head_dim)
    query_total = query_own + jnp.einsum(
        "qpd,ph->qhd", returned, send_map.astype(jnp.bfloat16), preferred_element_type=jnp.float32
    )
    query_done = query_total.astype(jnp.bfloat16)
    key_done = (key_own + key_total).astype(jnp.bfloat16)
    value_done = (value_own + value_total).astype(jnp.bfloat16)
    query_flat = query_done.reshape(row_count, head_count * head_dim)
    input_local = inputs[0]
    weight_grad = lax.psum_scatter(
        lax.dot_general(
            input_local, query_flat, (((0,), (0,)), ((), ())), preferred_element_type=jnp.float32
        ),
        ("dp", "ctx"),
        scatter_dimension=0,
        tiled=True,
    )
    return (query_done[None], key_done[None], value_done[None], weight_grad)


def solution(mesh):
    return jax.shard_map(
        per_device,
        mesh=mesh,
        in_specs=(
            P("dp", "ctx", None, None),
            P("dp", "ctx", None, None),
            P("dp", "ctx", None, None),
            P("dp", "ctx", None, None),
            P("dp", "ctx", None, None),
            P("dp", None, "ctx"),
            P("dp", "ctx", None, None),
            P("dp", "ctx", None),
        ),
        out_specs=(
            P("dp", "ctx", None, None),
            P("dp", "ctx", None, None),
            P("dp", "ctx", None, None),
            P(("dp", "ctx"), None),
        ),
        check_vma=False,
    )
```

profile of v0, /device:TPU:1, one launch (start us, length us, event | category | flops | bytes accessed | tf_op | source)
XLA Modules:
  0.0 1613.1 jit_solution(17452677236296090083)
XLA Ops:
  7.2 25.9 %all_gather.3 = s32[1,32,16,3]{2,0,3,1:T(1,128)S(1)} all-gather(s32[1,1,16,3]{2,0,3,1:T(1,128)} %bitcast.171), channel_id=1, replica_groups=mesh['dp'=8,'ctx'=32] {'ctx'}, dimensions={1}, use_global_device_ids=true | all-gather | bytes 6336 | tf_op jit(solution)/shard_map/all_gather | solution.py:49
  35.5 1.5 fusion.49
  39.0 4.9 all-to-all-start.1
  44.3 2.1 gather_fusion.5
  46.4 2.1 gather_fusion.2
  48.5 4.7 broadcast_select_fusion.3
  53.2 35.9 %all_to_all.20 = bf16[128,32,2,128]{3,0,2,1:T(8,128)(2,1)} all-to-all(bf16[128,32,2,128]{3,0,2,1:T(8,128)(2,1)} %bitcast.159), channel_id=1, replica_groups=mesh['dp'=8,'ctx'=32] {'ctx'}, dimensions={1} | all-to-all | bytes 4194304 | tf_op jit(solution)/shard_map/all_to_all | solution.py:72
  89.1 4.9 all-to-all-start.2
  94.0 1.4 multiply_reduce_fusion
  96.2 2.3 copy_bitcast_fusion
  98.5 23.5 %all-to-all-done.2 = bf16[128,32,2,128]{3,0,2,1:T(8,128)(2,1)} async-done(((bf16[128,32,2,128]{3,0,2,1:T(8,128)(2,1)}), bf16[128,32,2,128]{3,0,2,1:T(8,128)(2,1)}, u32[]{:S(2)}, u32[]{:S(2)}) %all-to-all-start.2) | async-done | bytes 2097184 | tf_op jit(solution)/shard_map/all_to_all | solution.py:73
  122.0 1.8 broadcast_in_dim.82
  123.8 118.6 %while.18 = (s32[]{:T(128)}, f32[128,16,128]{2,1,0:T(8,128)}, f32[128,16,128]{2,1,0:T(8,128)S(1)}, bf16[128,64,128]{0,2,1:T(8,128)(2,1)}, f32[64,16]{1,0:T(8,128...) while((s32[]{:T(128)}, f32[128,16,128]{2,1,0:T(8,128)}, ...), condition=%wide.region_6.10_spmd.clone, body=%wide.region_5.9_spmd.clone.sunk | while | flops 220857392 | bytes 16028254 | solution.py:145
  124.0 1.6 gather_fusion
  125.7 1.7 gather_fusion.1
  134.3 2.1 fusion.109
  137.7 1.6 gather_fusion
  139.4 1.7 gather_fusion.1
  148.1 3.3 fusion.109
  152.7 1.6 gather_fusion
  154.4 1.7 gather_fusion.1
  163.0 3.3 fusion.109
  167.7 1.6 gather_fusion
  169.4 1.7 gather_fusion.1
  171.1 1.3 fusion.106
  178.0 3.3 fusion.109
  182.7 1.6 gather_fusion
  184.3 1.7 gather_fusion.1
  186.1 1.3 fusion.106
  193.0 3.3 fusion.109
  197.7 1.6 gather_fusion
  199.3 1.7 gather_fusion.1
  208.0 3.3 fusion.109
  212.7 1.6 gather_fusion
  214.3 1.7 gather_fusion.1
  223.0 3.3 fusion.109
  227.7 1.6 gather_fusion
  229.3 1.7 gather_fusion.1
  238.0 3.3 fusion.109
  242.5 6.2 copy.160
  248.6 7.1 all-to-all-start.3
  255.9 1.6 fusion.42
  259.0 24.7 %all-to-all-done.3 = bf16[128,32,2,128]{3,2,0,1:T(2,128)(2,1)} async-done(((bf16[128,32,2,128]{3,2,0,1:T(2,128)(2,1)}), bf16[128,32,2,128]{3,2,0,1:T(2,128)(2,1)}, u32[]{:S(2)}, u32[]{:S(2)}) %all-to-all-start.3) | async-done | bytes 2097184 | tf_op jit(solution)/shard_map/all_to_all | solution.py:148
  283.7 3.9 copy.161
  290.3 9.1 convolution_bitcast_fusion.3
  299.4 17.6 %copy.187 = f32[2048,2048]{1,0:T(8,128)} copy(f32[2048,2048]{0,1:T(8,128)} %convolution_bitcast_fusion.3) | data formatting | bytes 33554432
  317.1 1.9 fusion.47
  323.0 1283.3 %reduce-scatter.4.cloned.1.call-done = f32[8,2048]{1,0:T(8,128)} async-done(((f32[2048,2048]{1,0:T(8,128)}), f32[8,2048]{1,0:T(8,128)}) %reduce-scatter.4.cloned.1.call-update) | async-done | bytes 65552
  (190 shorter events, 76.3 us)
Async XLA Ops:
  7.2 283.1 %copy-start = (bf16[1,128,2048]{2,1,0:T(8,128)(2,1)S(1)}, bf16[1,128,2048]{2,1,0:T(8,128)(2,1)}, u32[]{:S(2)}) copy-start(bf16[1,128,2048]{2,1,0:T(8,128)(2,1)} %param.23) | copy-start | bytes 1572868
  7.2 36.8 %copy-start.3 = (bf16[1,128,16,128]{3,2,1,0:T(8,128)(2,1)S(1)}, bf16[1,128,16,128]{3,2,1,0:T(8,128)(2,1)}, u32[]{:S(2)}) copy-start(bf16[1,128,16,128]{3,2,1,0:T(8,128)(2,1)} %param.20) | copy-start | bytes 1572868
  7.2 30.5 %copy-start.2 = (f32[1,16,128]{2,1,0:T(8,128)S(1)}, f32[1,16,128]{2,1,0:T(8,128)}, u32[]{:S(2)}) copy-start(f32[1,16,128]{2,1,0:T(8,128)} %param.21) | copy-start | bytes 24580
  33.3 10.8 copy-start.7
  39.0 14.2 all-to-all-start.1
  89.1 7.0 copy-start.10
  89.1 32.9 %all-to-all-start.2 = ((bf16[128,32,2,128]{3,0,2,1:T(8,128)(2,1)}), bf16[128,32,2,128]{3,0,2,1:T(8,128)(2,1)}, u32[]{:S(2)}, u32[]{:S(2)}) async-start(bf16[128,32,2,128]{3,0,2,1:T(8,128)(2,1)} %bitcast.158), calls=%async_computation.2 | async-start | bytes 4194304 | tf_op jit(solution)/shard_map/all_to_all | solution.py:73
  125.7 1.8 copy-start.4
  134.3 2.1 copy-start.5
  139.4 1.8 copy-start.4
  148.0 3.4 copy-start.5
  154.4 1.8 copy-start.4
  163.0 3.4 copy-start.5
  169.4 1.8 copy-start.4
  178.0 3.4 copy-start.5
  184.3 1.8 copy-start.4
  193.0 3.4 copy-start.5
  199.3 1.8 copy-start.4
  208.0 3.4 copy-start.5
  214.3 1.8 copy-start.4
  223.0 3.4 copy-start.5
  229.3 1.8 copy-start.4
  238.0 3.4 copy-start.5
  248.6 7.2 copy-start.8
  248.6 35.0 %all-to-all-start.3 = ((bf16[128,32,2,128]{3,2,0,1:T(2,128)(2,1)}), bf16[128,32,2,128]{3,2,0,1:T(2,128)(2,1)}, u32[]{:S(2)}, u32[]{:S(2)}) async-start(bf16[128,32,2,128]{3,2,0,1:T(2,128)(2,1)} %copy.160), calls=%async_computation.3 | async-start | bytes 4194304 | tf_op jit(solution)/shard_map/all_to_all | solution.py:148
  255.7 2.8 copy-start.11
  255.7 1350.6 %reduce-scatter.4.cloned.1.call-start = ((), (), s32[]{:S(2)}) async-start(), calls=%async_computation.5 | async-start | bytes 16842752
  257.5 1.0 copy-start.6
  287.6 1.0 copy-start.12
  317.0 3.1 copy-start.1
  317.1 3.1 copy-start.9
Sparse Core Ops, SparseCore 0:
  317.2 1289.0 reduce-scatter.3
where the time goes:
time: 1620 us; the launch traced here: 1610 us
  waiting for transfers between devices  1330 us (82%)
  matrix products  101 us (6%)
  local copies, waits for them, and re-layouts  76 us (5%)
  blocking collectives  61.8 us (4%)
  starting transfers between devices  16.9 us (1%)
    unnamed x2, waiting for transfers between devices  1280 us
    all_to_all x1, blocking collectives, per_device(): lax.all_to_all(query_slots, 'ctx', split_axis=1, concat_axis=1, tiled=True)  35.9 us
  transfers between devices with their start and end apart: 4, of which 3 were waited for; matrix products, arithmetic and copies ran while one was open for 1% of the time, Pallas kernels for 0%

commit v1 on v0

v1 whole, which is shorter than its diff:
```python
import functools

import jax
import jax.numpy as jnp
from jax import lax
from jax.experimental import pallas as pl
from jax.experimental.pallas import tpu as pltpu
from jax.sharding import PartitionSpec as P

CAP = 2
MESH = pl.DeviceIdType.MESH
DEAD = 1e30
NT = (((1,), (1,)), ((), ()))
NN = (((1,), (0,)), ((), ()))
TN = (((0,), (0,)), ((), ()))


def mm(a, b, dims):
    return lax.dot_general(a, b, dims, preferred_element_type=jnp.float32)


def pair_grads(query, grad, key, value, lse, delta, scale, keep=None):
    scores = mm(key, query, NT) * scale
    probs = jnp.exp(scores - lse)
    if keep is not None:
        probs = jnp.where(keep, probs, 0.0)
    dprobs = mm(value, grad, NT)
    dscores = (probs * (dprobs - delta)).astype(jnp.bfloat16)
    query_part = mm(dscores, key, TN) * scale
    key_part = mm(dscores, query, NN) * scale
    value_part = mm(probs.astype(jnp.bfloat16), grad, NN)
    return query_part, key_part, value_part


def kernel(
    nd,
    nc,
    q_ref,
    k_ref,
    v_ref,
    g_ref,
    x_ref,
    lse_ref,
    delta_ref,
    ids_ref,
    head_ref,
    live_ref,
    pos_ref,
    qg_ref,
    dk_ref,
    dv_ref,
    wg_ref,
    ids_in,
    ids_smem,
    last_smem,
    fwd_out,
    fwd_in,
    stat_out,
    stat_in,
    ret_out,
    ret_in,
    own_q,
    arena_k,
    arena_v,
    x_all,
    qg_all,
    w_out,
    w_in,
    w_sum,
    w_fin,
    local_sem,
    id_send,
    id_recv,
    fwd_send,
    fwd_recv,
    stat_send,
    stat_recv,
    ret_send,
    ret_recv,
    up_send,
    up_recv,
    down_send,
    down_recv,
    sib_send,
    sib_recv,
    qg_send,
    qg_recv,
    w_send,
    w_recv,
    f_send,
    f_recv,
):
    heads, rows, depth = q_ref.shape
    scale = depth ** (-0.5)
    width = x_ref.shape[1]
    span = width // nd
    me = lax.axis_index("ctx")
    zd = lax.axis_index("dp")
    core = lax.rem(me, 2)
    chip = me // 2
    chips = nc // 2
    mine = 2 * zd + core

    def peer(j):
        return {"dp": zd, "ctx": j}

    def group_peer(t):
        return {"dp": t // 2, "ctx": 2 * chip + lax.rem(t, 2)}

    barrier = pltpu.get_barrier_semaphore()

    @pl.loop(0, nc)
    def _(j):
        @pl.when(j != me)
        def _():
            pl.semaphore_signal(barrier, inc=1, device_id=peer(j), device_id_type=MESH)

    @pl.loop(0, 2 * nd)
    def _(t):
        @pl.when(t // 2 != zd)
        def _():
            pl.semaphore_signal(barrier, inc=1, device_id=group_peer(t), device_id_type=MESH)

    def x_rows(shard, which):
        return pl.ds(pl.multiple_of((2 * shard + which) * rows, rows), rows)

    seat = pltpu.make_async_copy(x_ref, x_all.at[x_rows(zd, core)], local_sem)
    seat.start()

    @pl.loop(0, me)
    def _(j):
        for s in range(CAP):
            h = head_ref[j, s]
            fwd_out[j, s, 0] = q_ref[h]
            fwd_out[j, s, 1] = g_ref[h]
            alive = live_ref[j, s] > 0
            stat_out[j, pl.ds(s, 1), :] = jnp.where(alive, lse_ref[pl.ds(h, 1), :], DEAD)
            stat_out[j, pl.ds(CAP + s, 1), :] = delta_ref[pl.ds(h, 1), :]

    seat.wait()
    pl.semaphore_wait(barrier, (nc - 1) + 2 * (nd - 1))

    def id_copy(src, j, dst):
        return pltpu.make_async_remote_copy(
            src_ref=ids_ref,
            dst_ref=ids_in.at[src],
            send_sem=id_send.at[j],
            recv_sem=id_recv.at[src],
            device_id=peer(dst),
            device_id_type=MESH,
        )

    def fwd_copy(src, j, dst):
        return pltpu.make_async_remote_copy(
            src_ref=fwd_out.at[j],
            dst_ref=fwd_in.at[src],
            send_sem=fwd_send.at[j],
            recv_sem=fwd_recv.at[src],
            device_id=peer(dst),
            device_id_type=MESH,
        )

    def stat_copy(src, j, dst):
        return pltpu.make_async_remote_copy(
            src_ref=stat_out.at[j],
            dst_ref=stat_in.at[src],
            send_sem=stat_send.at[j],
            recv_sem=stat_recv.at[src],
            device_id=peer(dst),
            device_id_type=MESH,
        )

    def ret_copy(src, j, dst):
        return pltpu.make_async_remote_copy(
            src_ref=ret_out.at[j],
            dst_ref=ret_in.at[pl.ds(CAP * src, CAP)],
            send_sem=ret_send.at[j],
            recv_sem=ret_recv.at[src],
            device_id=peer(dst),
            device_id_type=MESH,
        )

    ups = nd // 2
    downs = nd - 1 - ups

    def up_copy(shard, s):
        return pltpu.make_async_remote_copy(
            src_ref=x_all.at[x_rows(shard, core)],
            dst_ref=x_all.at[x_rows(shard, core)],
            send_sem=up_send.at[s],
            recv_sem=up_recv.at[s],
            device_id={"dp": lax.rem(zd + 1, nd), "ctx": me},
            device_id_type=MESH,
        )

    def down_copy(shard, s):
        return pltpu.make_async_remote_copy(
            src_ref=x_all.at[x_rows(shard, core)],
            dst_ref=x_all.at[x_rows(shard, core)],
            send_sem=down_send.at[s],
            recv_sem=down_recv.at[s],
            device_id={"dp": lax.rem(zd + nd - 1, nd), "ctx": me},
            device_id_type=MESH,
        )

    def sib_copy(shard, which, n):
        return pltpu.make_async_remote_copy(
            src_ref=x_all.at[x_rows(shard, which)],
            dst_ref=x_all.at[x_rows(shard, which)],
            send_sem=sib_send.at[n],
            recv_sem=sib_recv.at[n],
            device_id=peer(2 * chip + 1 - core),
            device_id_type=MESH,
        )

    def below(s):
        return lax.rem(zd + nd - s, nd)

    def above(s):
        return lax.rem(zd + s, nd)

    def relay(k):
        if k == 0:
            up_copy(zd, 0).start()
            if downs:
                down_copy(zd, 0).start()
            sib_copy(zd, core, 0).start()
            return
        up_copy(below(k), k - 1).wait_recv()
        if k < ups:
            up_copy(below(k), k).start()
        sib_copy(below(k), core, k).start()
        if k <= downs:
            down_copy(above(k), k - 1).wait_recv()
            if k < downs:
                down_copy(above(k), k).start()
            sib_copy(above(k), core, ups + k).start()

    @pl.loop(0, me)
    def _(n):
        j = me - 1 - n
        id_copy(me, j, j).start()

    @pl.loop(0, me)
    def _(n):
        j = me - 1 - n
        stat_copy(me, j, j).start()
        fwd_copy(me, j, j).start()

    relay(0)

    key_pos = lax.broadcasted_iota(jnp.int32, (rows, rows), 0)
    query_pos = lax.broadcasted_iota(jnp.int32, (rows, rows), 1)
    causal = key_pos <= query_pos

    @pl.loop(0, heads // 2)
    def _(n):
        for s in range(2):
            h = 2 * n + s
            query_part, key_part, value_part = pair_grads(
                q_ref[h],
                g_ref[h],
                k_ref[h],
                v_ref[h],
                lse_ref[pl.ds(h, 1), :],
                delta_ref[pl.ds(h, 1), :],
                scale,
                causal,
            )
            own_q[h] = query_part
            arena_k[h] = key_part
            arena_v[h] = value_part

    for h in range(heads):
        last_smem[h] = h

    @pl.loop(me + 1, nc)
    def _(i):
        id_copy(i, i, i).wait_recv()

    to_smem = pltpu.make_async_copy(ids_in, ids_smem, local_sem)
    to_smem.start()
    to_smem.wait()

    @pl.loop(1, nc)
    def _(step):
        i = me + step

        @pl.when(i < nc)
        def _():
            stat_copy(i, i, i).wait_recv()
            fwd_copy(i, i, i).wait_recv()
            for s in range(CAP):
                h = ids_smem[i, 0, CAP * me + s]
                row = heads + CAP * i + s
                query_part, key_part, value_part = pair_grads(
                    fwd_in[i, s, 0],
                    fwd_in[i, s, 1],
                    k_ref[h],
                    v_ref[h],
                    stat_in[i, pl.ds(s, 1), :],
                    stat_in[i, pl.ds(CAP + s, 1), :],
                    scale,
                )
                ret_out[i, s] = query_part.astype(jnp.bfloat16)
                before = last_smem[h]
                arena_k[row] = arena_k[before] + key_part
                arena_v[row] = arena_v[before] + value_part
                for t in range(heads):
                    last_smem[t] = jnp.where(h == t, row, last_smem[t])
            ret_copy(me, i, i).start()

        for k in range(1, ups + 1):

            @pl.when(step == max(1, k * nc // (2 * ups)))
            def _():
                relay(k)

    @pl.loop(0, heads)
    def _(h):
        at = last_smem[h]
        dk_ref[h] = arena_k[at].astype(jnp.bfloat16)
        dv_ref[h] = arena_v[at].astype(jnp.bfloat16)

    ret_in[CAP * nc] = jnp.zeros((rows, depth), jnp.bfloat16)

    @pl.loop(0, me)
    def _(j):
        ret_copy(j, j, j).wait_recv()

    topk = pos_ref.shape[1]

    @pl.loop(0, heads)
    def _(h):
        total = own_q[h]
        for e in range(topk):
            total = total + ret_in[pos_ref[h, e]].astype(jnp.float32)
        qg_ref[h] = total.astype(jnp.bfloat16)

    def qg_copy(src, t, dst):
        return pltpu.make_async_remote_copy(
            src_ref=qg_ref.at[t],
            dst_ref=qg_all.at[pl.ds(pl.multiple_of(src * rows, rows), rows)],
            send_sem=qg_send.at[t],
            recv_sem=qg_recv.at[src],
            device_id=group_peer(dst),
            device_id_type=MESH,
        )

    @pl.loop(0, 2 * nd)
    def _(t):
        @pl.when(t != mine)
        def _():
            qg_copy(mine, t, t).start()

    qg_all[pl.ds(pl.multiple_of(mine * rows, rows), rows), :] = qg_ref[mine]

    for n in range(nd):
        shard = zd if n == 0 else (below(n) if n <= ups else above(n - ups))
        sib_copy(shard, 1 - core, n).wait_recv()

    @pl.loop(0, 2 * nd)
    def _(t):
        @pl.when(t != mine)
        def _():
            qg_copy(t, t, t).wait_recv()

    flipped = qg_all[...].T

    @pl.loop(0, nd)
    def _(r):
        part = mm(flipped, x_all[:, pl.ds(pl.multiple_of(r * span, span), span)], NN)
        w_out[:, r] = part.T.astype(jnp.bfloat16).reshape(chips, span // chips, depth)

    def w_copy(src, t, dst):
        return pltpu.make_async_remote_copy(
            src_ref=w_out.at[t],
            dst_ref=w_in.at[src],
            send_sem=w_send.at[t],
            recv_sem=w_recv.at[src],
            device_id=peer(2 * dst + core),
            device_id_type=MESH,
        )

    @pl.loop(1, chips)
    def _(n):
        t = lax.rem(chip + n, chips)
        w_copy(chip, t, t).start()

    w_in[chip] = w_out[chip]

    @pl.loop(1, chips)
    def _(n):
        t = lax.rem(chip + n, chips)
        w_copy(t, t, t).wait_recv()

    w_sum[...] = jnp.sum(w_in[...].astype(jnp.float32), 0)

    def f_copy(src, t, dst):
        return pltpu.make_async_remote_copy(
            src_ref=w_sum.at[t // 2, pl.ds(pl.multiple_of(8 * lax.rem(t, 2), 8), 8)],
            dst_ref=w_fin.at[src],
            send_sem=f_send.at[t],
            recv_sem=f_recv.at[src],
            device_id=group_peer(dst),
            device_id_type=MESH,
        )

    @pl.loop(0, 2 * nd)
    def _(t):
        @pl.when(t != mine)
        def _():
            f_copy(mine, t, t).start()

    w_fin[mine] = w_sum[zd, pl.ds(pl.multiple_of(8 * core, 8), 8), :]

    @pl.loop(0, me)
    def _(j):
        id_copy(me, j, j).wait_send()
        stat_copy(me, j, j).wait_send()
        fwd_copy(me, j, j).wait_send()

    @pl.loop(me + 1, nc)
    def _(i):
        ret_copy(me, i, i).wait_send()

    for s in range(ups):
        up_copy(zd, s).wait_send()
    for s in range(downs):
        down_copy(zd, s).wait_send()
    for n in range(nd):
        sib_copy(zd, core, n).wait_send()

    @pl.loop(1, chips)
    def _(n):
        t = lax.rem(chip + n, chips)
        w_copy(chip, t, t).wait_send()

    @pl.loop(0, 2 * nd)
    def _(t):
        @pl.when(t != mine)
        def _():
            qg_copy(mine, t, t).wait_send()
            f_copy(mine, t, t).wait_send()
            f_copy(t, t, t).wait_recv()

    for t in range(2 * nd):
        wg_ref[:, t * depth : (t + 1) * depth] = w_fin[t]


def per_device(nd, nc, queries, key_rows, value_rows, attn_out, out_grad, log_sums, chosen, inputs):
    rows, heads, depth = queries.shape[1:]
    width = inputs.shape[2]
    topk = chosen.shape[3]
    me = lax.axis_index("ctx")

    def by_head(array):
        return jnp.swapaxes(array[0], 0, 1)

    delta = jnp.sum(out_grad[0].astype(jnp.float32) * attn_out[0].astype(jnp.float32), -1).T
    flat = chosen.reshape(heads * topk)
    live = flat < me
    order = jnp.arange(heads * topk, dtype=jnp.int32)
    same = (flat[:, None] == flat[None, :]) & live[None, :] & (order[None, :] < order[:, None])
    rank = jnp.sum(same.astype(jnp.int32), -1)
    spot = jnp.where(live, CAP * flat + rank, CAP * nc)
    hit = (spot[None, :] == jnp.arange(128, dtype=jnp.int32)[:, None]) & live[None, :]
    ids = jnp.sum(jnp.where(hit, order[None, :] // topk, 0), -1)
    alive = jnp.sum(hit.astype(jnp.int32), -1)
    slots = nc * CAP
    bf16, f32 = jnp.bfloat16, jnp.float32
    chips = nc // 2
    span = width // nd
    vmem = pl.BlockSpec(memory_space=pltpu.VMEM)
    smem = pl.BlockSpec(memory_space=pltpu.SMEM)
    dma = pltpu.SemaphoreType.DMA
    ups = nd // 2
    downs = nd - 1 - ups
    outs = pl.pallas_call(
        functools.partial(kernel, nd, nc),
        out_shape=(
            jax.ShapeDtypeStruct((heads, rows, depth), bf16),
            jax.ShapeDtypeStruct((heads, rows, depth), bf16),
            jax.ShapeDtypeStruct((heads, rows, depth), bf16),
            jax.ShapeDtypeStruct((8, heads * depth), f32),
        ),
        in_specs=[vmem] * 8 + [smem] * 3,
        out_specs=(vmem,) * 4,
        scratch_shapes=[
            pltpu.VMEM((nc, 1, 128), jnp.int32),
            pltpu.SMEM((nc, 1, 128), jnp.int32),
            pltpu.SMEM((heads,), jnp.int32),
            pltpu.VMEM((nc, CAP, 2, rows, depth), bf16),
            pltpu.VMEM((nc, CAP, 2, rows, depth), bf16),
            pltpu.VMEM((nc, 8, 128), f32),
            pltpu.VMEM((nc, 8, 128), f32),
            pltpu.VMEM((nc, CAP, rows, depth), bf16),
            pltpu.VMEM((slots + 1, rows, depth), bf16),
            pltpu.VMEM((heads, rows, depth), f32),
            pltpu.VMEM((heads + slots, rows, depth), f32),
            pltpu.VMEM((heads + slots, rows, depth), f32),
            pltpu.VMEM((2 * nd * rows, width), bf16),
            pltpu.VMEM((2 * nd * rows, depth), bf16),
            pltpu.VMEM((chips, nd, span // chips, depth), bf16),
            pltpu.VMEM((chips, nd, span // chips, depth), bf16),
            pltpu.VMEM((nd, span // chips, depth), f32),
            pltpu.VMEM((2 * nd, 8, depth), f32),
            dma(()),
            dma((nc,)),
            dma((nc,)),
            dma((nc,)),
            dma((nc,)),
            dma((nc,)),
            dma((nc,)),
            dma((nc,)),
            dma((nc,)),
            dma((ups,)),
            dma((ups,)),
            dma((max(downs, 1),)),
            dma((max(downs, 1),)),
            dma((nd,)),
            dma((nd,)),
            dma((2 * nd,)),
            dma((2 * nd,)),
            dma((chips,)),
            dma((chips,)),
            dma((2 * nd,)),
            dma((2 * nd,)),
        ],
        compiler_params=pltpu.CompilerParams(
            collective_id=0, has_side_effects=True, vmem_limit_bytes=58 * 1024 * 1024
        ),
    )(
        by_head(queries),
        by_head(key_rows),
        by_head(value_rows),
        by_head(out_grad),
        inputs[0],
        log_sums[0],
        delta,
        ids[None],
        ids[:slots].reshape(nc, CAP),
        alive[:slots].reshape(nc, CAP),
        spot.reshape(heads, topk),
    )
    query_grad, key_grad, value_grad, weight_grad = outs
    return (
        jnp.swapaxes(query_grad, 0, 1)[None],
        jnp.swapaxes(key_grad, 0, 1)[None],
        jnp.swapaxes(value_grad, 0, 1)[None],
        weight_grad,
    )


def solution(mesh):
    nd, nc = mesh.shape["dp"], mesh.shape["ctx"]
    four = P("dp", "ctx", None, None)
    return jax.shard_map(
        functools.partial(per_device, nd, nc),
        mesh=mesh,
        in_specs=(four, four, four, four, four, P("dp", None, "ctx"), four, P("dp", "ctx", None)),
        out_specs=(four, four, four, P(("dp", "ctx"), None)),
        check_vma=False,
    )
```

time: 1620 us -> 137 us (0.08)
  waiting for transfers between devices: 1330 us -> 0 us
  Pallas kernels: 0 us -> 123 us
  matrix products: 101 us -> 0 us
  local copies, waits for them, and re-layouts: 76 us -> 10.2 us
  blocking collectives: 61.8 us -> 0 us
  starting transfers between devices: 16.9 us -> 0 us
    unnamed x2 -> x0, waiting for transfers between devices: 1280 us -> none
    pallas_call x0 -> x1, Pallas kernels: none -> 123 us  [per_device(): pl.pallas_call(functools.partial(kernel, nd, nc), out_shape=(jax.ShapeDty...]
    dot_general x64 -> x0, matrix products: 101 us -> none  [the longest x8 25.4 us: group_pass(): jnp.einsum('kgd,gh->khd', key_part, onehot_group, precision=lax.Precision...]
    all_to_all x3 -> x0, waiting for transfers between devices: 48.2 us -> none  [the longest x1 24.7 us: per_device(): lax.all_to_all(parts.reshape(row_count, block_count, CAP, head_dim), 'ctx...]
    all_to_all x1 -> x0, blocking collectives: 35.9 us -> none  [per_device(): lax.all_to_all(query_slots, 'ctx', split_axis=1, concat_axis=1, tiled=True)]
    gather x20 -> x0, local copies, waits for them, and re-layouts: 32.5 us -> none  [the longest x8 13.9 us: group_pass(): value_group = jnp.take(value_local, head_group, axis=1)]
    all_gather x1 -> x0, blocking collectives: 25.9 us -> none  [per_device(): chosen_all = lax.all_gather(chosen, 'ctx', axis=1, tiled=True)[0]]
    unnamed x28 -> x23, local copies, waits for them, and re-layouts: 23 us -> 5.92 us
  transfers between devices with their start and end apart: 4 -> 0, of which waited for: 3 -> 0; matrix products, arithmetic and copies ran while one was open for 1% -> 0% of each run, Pallas kernels for 0% -> 0%
where the time goes in v1:
time: 137 us
  Pallas kernels  123 us (90%)
  local copies, waits for them, and re-layouts  10.2 us (7%)
  other arithmetic  3.16 us (2%)
    pallas_call x1, Pallas kernels, per_device(): pl.pallas_call(functools.partial(kernel, nd, nc), out_shape=(jax.ShapeDty...  123 us
    unnamed x23, local copies, waits for them, and re-layouts  5.92 us

profile of v1, /device:TPU:1, one launch (start us, length us, event | category | flops | bytes accessed | tf_op | source)
XLA Modules:
  0.0 136.7 jit_solution(10617327748921042448)
XLA Ops:
  0.6 0.0 copy-start.7
  0.6 0.7 copy-done.7
  1.3 0.1 copy.45
  1.4 0.1 copy.46
  1.5 0.0 copy-start
  1.5 0.0 copy-start.3
  1.5 2.2 %fusion = f32[128,16]{0,1:T(8,128)} fusion(bf16[1,128,16,128]{3,2,1,0:T(8,128)(2,1)} %param.11, bf16[1,128,16,128]{3,2,1,0:T(8,128)(2,1)} %param.12), kind=kLoop, calls=%fused_computation.1 | loop fusion | flops 1046528 | bytes 1056768 | tf_op jit(solution)/shard_map/reduce_sum | solution.py:460
  3.7 0.1 copy.39
  3.8 0.1 reshape.83
  3.9 0.2 convert_reduce_fusion.1
  4.1 0.1 convert_reduce_fusion
  4.2 0.0 copy-start.8
  4.2 0.1 reduce_sum.42
  4.3 0.6 fusion.3.pos_ref
  4.9 0.7 reshape.85.live_ref
  5.6 0.0 copy-done.8
  5.6 0.7 reshape.84.head_ref
  6.4 0.0 copy-done
  6.4 0.0 copy-done.3
  6.4 0.0 copy-start.4
  6.4 0.0 copy-start.5
  6.4 1.3 copy_bitcast_fusion.2
  7.7 0.0 copy-done.4
  7.7 0.0 copy-done.5
  7.7 1.3 copy_bitcast_fusion
  8.9 122.6 %shard_map.111 = (bf16[16,128,128]{2,1,0:T(8,128)(2,1)}, bf16[16,128,128]{2,1,0:T(8,128)(2,1)}, bf16[16,128,128]{2,1,0:T(8,128)(2,1)}, f32[8,2048]{1,0:T(8,128)}) custom-call(bf16[16,128,128]{2,1,0:T(8,128)(2,1)} %get-tuple-element.30.q_ref, bf16[16,128,128]{2,1,0:T(8,128)(2,1)} %get-tuple-element.29.k_ref, bf16[16,128,128]{2,1,0:T(8,128)(2,1)} %get-tuple-element.28.v_ref, ...), custom_call_target="tpu_custom_call" | custom-call | tf_op jit(solution)/shard_map/pallas_call | solution.py:479
  131.6 0.0 copy-start.2
  131.6 2.2 %copy.42 = bf16[1,128,16,128]{3,2,1,0:T(8,128)(2,1)} copy(bf16[1,128,16,128]{3,1,2,0:T(8,128)(2,1)} %bitcast.45) | data formatting | bytes 1048576
  133.8 0.0 copy-done.2
  133.8 0.0 copy-start.1
  133.8 1.1 copy.43
  135.0 0.0 copy-done.1
  135.0 0.0 copy-start.6
  135.0 1.1 copy.44
  136.1 0.0 copy-done.6
  136.1 0.6 copy.54
  (4 shorter events, 0.0 us)
Async XLA Ops:
  0.6 0.7 copy-start.7
  1.5 4.8 %copy-start = (bf16[1,128,16,128]{3,2,1,0:T(8,128)(2,1)S(1)}, bf16[1,128,16,128]{3,2,1,0:T(8,128)(2,1)}, u32[]{:S(2)}) copy-start(bf16[1,128,16,128]{3,2,1,0:T(8,128)(2,1)} %param.12) | copy-start | bytes 1572868
  1.5 4.8 %copy-start.3 = (bf16[1,128,16,128]{3,2,1,0:T(8,128)(2,1)S(1)}, bf16[1,128,16,128]{3,2,1,0:T(8,128)(2,1)}, u32[]{:S(2)}) copy-start(bf16[1,128,16,128]{3,2,1,0:T(8,128)(2,1)} %param.8) | copy-start | bytes 1572868
  4.2 1.4 %copy-start.8 = (s32[128]{0:T(128)}, s32[128]{0:T(128)S(1)}, u32[]{:S(2)}) copy-start(s32[128]{0:T(128)S(1)} %get-tuple-element.25) | copy-start | bytes 1540
  6.4 1.3 copy-start.4
  6.4 1.3 copy-start.5
  131.6 2.2 %copy-start.2 = (bf16[16,128,128]{2,1,0:T(8,128)(2,1)S(1)}, bf16[16,128,128]{2,1,0:T(8,128)(2,1)}, u32[]{:S(2)}) copy-start(bf16[16,128,128]{2,1,0:T(8,128)(2,1)} %get-tuple-element.9) | copy-start | bytes 1572868
  133.8 1.1 copy-start.1
  135.0 1.1 copy-start.6

commit v2 on v1

--- a/solution.py
+++ b/solution.py
@@ -35,21 +35,30 @@
 def kernel(
     nd,
     nc,
+    q_in,
+    k_in,
+    v_in,
+    o_in,
+    g_in,
+    x_ref,
+    lse_ref,
+    pick_ref,
+    qg_out,
+    dk_out,
+    dv_out,
+    wg_ref,
     q_ref,
     k_ref,
     v_ref,
     g_ref,
-    x_ref,
-    lse_ref,
-    delta_ref,
-    ids_ref,
-    head_ref,
-    live_ref,
-    pos_ref,
     qg_ref,
     dk_ref,
     dv_ref,
-    wg_ref,
+    delta_ref,
+    ids_ref,
+    pos_row,
+    head_ref,
+    pos_ref,
     ids_in,
     ids_smem,
     last_smem,
@@ -64,11 +73,13 @@
     arena_v,
     x_all,
     qg_all,
+    w_acc,
     w_out,
     w_in,
     w_sum,
     w_fin,
     local_sem,
+    table_sem,
     id_send,
     id_recv,
     fwd_send,
@@ -90,7 +101,8 @@
     f_send,
     f_recv,
 ):
-    heads, rows, depth = q_ref.shape
+    rows, heads, depth = q_in.shape
+    topk = pick_ref.shape[1]
     scale = depth ** (-0.5)
     width = x_ref.shape[1]
     span = width // nd
@@ -127,18 +139,57 @@
     seat = pltpu.make_async_copy(x_ref, x_all.at[x_rows(zd, core)], local_sem)
     seat.start()
 
-    @pl.loop(0, me)
-    def _(j):
-        for s in range(CAP):
-            h = head_ref[j, s]
-            fwd_out[j, s, 0] = q_ref[h]
-            fwd_out[j, s, 1] = g_ref[h]
-            alive = live_ref[j, s] > 0
-            stat_out[j, pl.ds(s, 1), :] = jnp.where(alive, lse_ref[pl.ds(h, 1), :], DEAD)
-            stat_out[j, pl.ds(CAP + s, 1), :] = delta_ref[pl.ds(h, 1), :]
-
+    lane = lax.broadcasted_iota(jnp.int32, (1, 128), 1)
+    block = lax.shift_right_logical(lane, 1)
+    slot = lane - 2 * block
+    earlier = jnp.where(block < me, block, -1)
+    ids = jnp.full((1, 128), heads, jnp.int32)
+    count = jnp.zeros((1, 128), jnp.int32)
+    picks = jnp.zeros((1, 128), jnp.int32)
+    for e in range(heads * topk):
+        target = pick_ref[e // topk, e % topk]
+        hit = earlier == target
+        ids = jnp.where(hit & (count == slot), e // topk, ids)
+        count = count + hit.astype(jnp.int32)
+        picks = jnp.where(lane == e, target, picks)
+    ids_ref[...] = ids
+    rank = jnp.zeros((1, 128), jnp.int32)
+    for e in range(heads * topk):
+        target = pick_ref[e // topk, e % topk]
+        rank = rank + ((picks == target) & (lane > e)).astype(jnp.int32)
+    pos_row[...] = jnp.where(picks < me, CAP * picks + rank, CAP * nc)
+    tables = [
+        pltpu.make_async_copy(ids_ref, head_ref, table_sem.at[0]),
+        pltpu.make_async_copy(pos_row, pos_ref, table_sem.at[1]),
+    ]
+    for table in tables:
+        table.start()
+
+    q_ref[...] = jnp.swapaxes(q_in[...], 0, 1)
+    g_ref[...] = jnp.swapaxes(g_in[...], 0, 1)
+    delta = jnp.zeros((heads, rows), jnp.float32)
+    for b in range(8):
+        part = slice(b * rows // 8, (b + 1) * rows // 8)
+        product = g_in[part].astype(jnp.float32) * o_in[part].astype(jnp.float32)
+        sums = jnp.sum(product, -1, keepdims=True)
+        shape = (rows // 8, heads, rows)
+        token = lax.broadcasted_iota(jnp.int32, shape, 0) + b * rows // 8
+        seat_of = lax.broadcasted_iota(jnp.int32, shape, 2)
+        delta = delta + jnp.sum(jnp.where(token == seat_of, sums, 0.0), 0)
+    delta_ref[...] = delta
+
+    for table in tables:
+        table.wait()
     seat.wait()
     pl.semaphore_wait(barrier, (nc - 1) + 2 * (nd - 1))
+
+    lines = nc // 8
+
+    def partner(n, sign):
+        a = n % lines
+        b = lax.rem(n // lines + 4 * lax.rem(a, 2), 8)
+        line = lax.rem(me // 8 + sign * a + lines, lines)
+        return 8 * line + lax.rem(lax.rem(me, 8) + sign * b + 8, 8)
 
     def id_copy(src, j, dst):
         return pltpu.make_async_remote_copy(
@@ -236,18 +287,28 @@
                 down_copy(above(k), k).start()
             sib_copy(above(k), core, ups + k).start()
 
-    @pl.loop(0, me)
+    relay(0)
+
+    @pl.loop(1, nc)
     def _(n):
-        j = me - 1 - n
-        id_copy(me, j, j).start()
-
-    @pl.loop(0, me)
-    def _(n):
-        j = me - 1 - n
-        stat_copy(me, j, j).start()
-        fwd_copy(me, j, j).start()
-
-    relay(0)
+        j = partner(n, -1)
+
+        @pl.when(j < me)
+        def _():
+            for s in range(CAP):
+                code = head_ref[0, CAP * j + s]
+                alive = code < heads
+                h = jnp.where(alive, code, 0)
+                fwd_out[j, s, 0] = q_ref[h]
+                fwd_out[j, s, 1] = g_ref[h]
+                stat_out[j, pl.ds(s, 1), :] = jnp.where(alive, lse_ref[pl.ds(h, 1), :], DEAD)
+                stat_out[j, pl.ds(CAP + s, 1), :] = delta_ref[pl.ds(h, 1), :]
+            id_copy(me, j, j).start()
+            stat_copy(me, j, j).start()
+            fwd_copy(me, j, j).start()
+
+    k_ref[...] = jnp.swapaxes(k_in[...], 0, 1)
+    v_ref[...] = jnp.swapaxes(v_in[...], 0, 1)
 
     key_pos = lax.broadcasted_iota(jnp.int32, (rows, rows), 0)
     query_pos = lax.broadcasted_iota(jnp.int32, (rows, rows), 1)
@@ -284,14 +345,15 @@
 
     @pl.loop(1, nc)
     def _(step):
-        i = me + step
-
-        @pl.when(i < nc)
+        i = partner(step, 1)
+
+        @pl.when(i > me)
         def _():
             stat_copy(i, i, i).wait_recv()
             fwd_copy(i, i, i).wait_recv()
             for s in range(CAP):
-                h = ids_smem[i, 0, CAP * me + s]
+                code = ids_smem[i, 0, CAP * me + s]
+                h = jnp.where(code < heads, code, 0)
                 row = heads + CAP * i + s
                 query_part, key_part, value_part = pair_grads(
                     fwd_in[i, s, 0],
@@ -316,85 +378,141 @@
             def _():
                 relay(k)
 
+    ret_in[CAP * nc] = jnp.zeros((rows, depth), jnp.bfloat16)
+
+    @pl.loop(0, me)
+    def _(j):
+        ret_copy(j, j, j).wait_recv()
+
+    def qg_copy(src, t, dst):
+        return pltpu.make_async_remote_copy(
+            src_ref=qg_ref.at[t],
+            dst_ref=qg_all.at[pl.ds(pl.multiple_of(src * rows, rows), rows)],
+            send_sem=qg_send.at[t],
+            recv_sem=qg_recv.at[src],
+            device_id=group_peer(dst),
+            device_id_type=MESH,
+        )
+
+    offsets = [0]
+    for k in range(1, nd // 2 + 1):
+        offsets += [k] if 2 * k == nd else [k, nd - k]
+
+    for offset in reversed(offsets):
+        for which in range(2):
+            h = 2 * above(offset) + which
+            total = own_q[h]
+            for e in range(topk):
+                total = total + ret_in[pos_ref[0, topk * h + e]].astype(jnp.float32)
+            qg_ref[h] = total.astype(jnp.bfloat16)
+            if offset:
+                qg_copy(mine, h, h).start()
+            else:
+
+                @pl.when(core != which)
+                def _():
+                    qg_copy(mine, h, h).start()
+
+                @pl.when(core == which)
+                def _():
+                    qg_all[pl.ds(pl.multiple_of(mine * rows, rows), rows), :] = qg_ref[h]
+
+    qg_out[...] = jnp.swapaxes(qg_ref[...], 0, 1)
+
     @pl.loop(0, heads)
     def _(h):
         at = last_smem[h]
         dk_ref[h] = arena_k[at].astype(jnp.bfloat16)
         dv_ref[h] = arena_v[at].astype(jnp.bfloat16)
 
-    ret_in[CAP * nc] = jnp.zeros((rows, depth), jnp.bfloat16)
-
-    @pl.loop(0, me)
-    def _(j):
-        ret_copy(j, j, j).wait_recv()
-
-    topk = pos_ref.shape[1]
-
-    @pl.loop(0, heads)
-    def _(h):
-        total = own_q[h]
-        for e in range(topk):
-            total = total + ret_in[pos_ref[h, e]].astype(jnp.float32)
-        qg_ref[h] = total.astype(jnp.bfloat16)
-
-    def qg_copy(src, t, dst):
-        return pltpu.make_async_remote_copy(
-            src_ref=qg_ref.at[t],
-            dst_ref=qg_all.at[pl.ds(pl.multiple_of(src * rows, rows), rows)],
-            send_sem=qg_send.at[t],
-            recv_sem=qg_recv.at[src],
-            device_id=group_peer(dst),
-            device_id_type=MESH,
-        )
+    dk_out[...] = jnp.swapaxes(dk_ref[...], 0, 1)
+    dv_out[...] = jnp.swapaxes(dv_ref[...], 0, 1)
+
+    for n in range(nd):
+        shard = zd if n == 0 else (below(n) if n <= ups else above(n - ups))
+        sib_copy(shard, 1 - core, n).wait_recv()
+
+    def add_chip(shard, r):
+        tokens = pl.ds(pl.multiple_of(2 * shard * rows, 2 * rows), 2 * rows)
+        columns = pl.ds(pl.multiple_of(r * span, span), span)
+        return mm(qg_all[tokens, :], x_all[tokens, columns], TN)
+
+    def w_copy(src, t, dst, half):
+        part = pl.ds(half * (nd // 2), nd // 2)
+        return pltpu.make_async_remote_copy(
+            src_ref=w_out.at[t, part],
+            dst_ref=w_in.at[src, part],
+            send_sem=w_send.at[half, t],
+            recv_sem=w_recv.at[half, src],
+            device_id=peer(2 * dst + core),
+            device_id_type=MESH,
+        )
+
+    wide = chips // lines
+
+    def chip_partner(n, sign):
+        a = n % lines
+        b = lax.rem(n // lines + (wide // 2) * lax.rem(a, 2), wide)
+        line = lax.rem(chip // wide + sign * a + lines, lines)
+        return wide * line + lax.rem(lax.rem(chip, wide) + sign * b + wide, wide)
+
+    for place, offset in enumerate(offsets):
+        shard = above(offset)
+        for which in range(2):
+            t = 2 * shard + which
+            if offset:
+                qg_copy(t, t, t).wait_recv()
+            else:
+
+                @pl.when(core != which)
+                def _():
+                    qg_copy(t, t, t).wait_recv()
+
+        if place < nd - 1:
+
+            @pl.loop(0, nd)
+            def _(r):
+                part = add_chip(shard, r)
+                w_acc[r] = part if place == 0 else w_acc[r] + part
+
+            if place == 0:
+
+                @pl.loop(0, nc)
+                def _(j):
+                    @pl.when(j < me)
+                    def _():
+                        id_copy(me, j, j).wait_send()
+                        stat_copy(me, j, j).wait_send()
+                        fwd_copy(me, j, j).wait_send()
+
+                    @pl.when(j > me)
+                    def _():
+                        ret_copy(me, j, j).wait_send()
+
+                for s in range(ups):
+                    up_copy(zd, s).wait_send()
+                for s in range(downs):
+                    down_copy(zd, s).wait_send()
+                for n in range(nd):
+                    sib_copy(zd, core, n).wait_send()
+        else:
+            for half in range(2):
+
+                @pl.loop(half * (nd // 2), (half + 1) * (nd // 2))
+                def _(r):
+                    part = w_acc[r] + add_chip(shard, r)
+                    w_out[:, r] = part.T.astype(jnp.bfloat16).reshape(chips, span // chips, depth)
+
+                @pl.loop(1, chips)
+                def _(n):
+                    t = chip_partner(n, -1)
+                    w_copy(chip, t, t, half).start()
 
     @pl.loop(0, 2 * nd)
     def _(t):
         @pl.when(t != mine)
         def _():
-            qg_copy(mine, t, t).start()
-
-    qg_all[pl.ds(pl.multiple_of(mine * rows, rows), rows), :] = qg_ref[mine]
-
-    for n in range(nd):
-        shard = zd if n == 0 else (below(n) if n <= ups else above(n - ups))
-        sib_copy(shard, 1 - core, n).wait_recv()
-
-    @pl.loop(0, 2 * nd)
-    def _(t):
-        @pl.when(t != mine)
-        def _():
-            qg_copy(t, t, t).wait_recv()
-
-    flipped = qg_all[...].T
-
-    @pl.loop(0, nd)
-    def _(r):
-        part = mm(flipped, x_all[:, pl.ds(pl.multiple_of(r * span, span), span)], NN)
-        w_out[:, r] = part.T.astype(jnp.bfloat16).reshape(chips, span // chips, depth)
-
-    def w_copy(src, t, dst):
-        return pltpu.make_async_remote_copy(
-            src_ref=w_out.at[t],
-            dst_ref=w_in.at[src],
-            send_sem=w_send.at[t],
-            recv_sem=w_recv.at[src],
-            device_id=peer(2 * dst + core),
-            device_id_type=MESH,
-        )
-
-    @pl.loop(1, chips)
-    def _(n):
-        t = lax.rem(chip + n, chips)
-        w_copy(chip, t, t).start()
-
-    w_in[chip] = w_out[chip]
-
-    @pl.loop(1, chips)
-    def _(n):
-        t = lax.rem(chip + n, chips)
-        w_copy(t, t, t).wait_recv()
-
-    w_sum[...] = jnp.sum(w_in[...].astype(jnp.float32), 0)
+            qg_copy(mine, t, t).wait_send()
 
     def f_copy(src, t, dst):
         return pltpu.make_async_remote_copy(
@@ -406,41 +524,34 @@
             device_id_type=MESH,
         )
 
+    for half in range(2):
+        part = pl.ds(half * (nd // 2), nd // 2)
+
+        def add_part(n, total):
+            t = chip_partner(n, 1)
+            w_copy(t, t, t, half).wait_recv()
+            return total + w_in[t, part].astype(jnp.float32)
+
+        w_sum[part] = lax.fori_loop(1, chips, add_part, w_out[chip, part].astype(jnp.float32))
+
+        @pl.loop(half * nd, (half + 1) * nd)
+        def _(t):
+            @pl.when(t != mine)
+            def _():
+                f_copy(mine, t, t).start()
+
+    w_fin[mine] = w_sum[zd, pl.ds(pl.multiple_of(8 * core, 8), 8), :]
+
+    @pl.loop(1, chips)
+    def _(n):
+        t = chip_partner(n, -1)
+        w_copy(chip, t, t, 0).wait_send()
+        w_copy(chip, t, t, 1).wait_send()
+
     @pl.loop(0, 2 * nd)
     def _(t):
         @pl.when(t != mine)
         def _():
-            f_copy(mine, t, t).start()
-
-    w_fin[mine] = w_sum[zd, pl.ds(pl.multiple_of(8 * core, 8), 8), :]
-
-    @pl.loop(0, me)
-    def _(j):
-        id_copy(me, j, j).wait_send()
-        stat_copy(me, j, j).wait_send()
-        fwd_copy(me, j, j).wait_send()
-
-    @pl.loop(me + 1, nc)
-    def _(i):
-        ret_copy(me, i, i).wait_send()
-
-    for s in range(ups):
-        up_copy(zd, s).wait_send()
-    for s in range(downs):
-        down_copy(zd, s).wait_send()
-    for n in range(nd):
-        sib_copy(zd, core, n).wait_send()
-
-    @pl.loop(1, chips)
-    def _(n):
-        t = lax.rem(chip + n, chips)
-        w_copy(chip, t, t).wait_send()
-
-    @pl.loop(0, 2 * nd)
-    def _(t):
-        @pl.when(t != mine)
-        def _():
-            qg_copy(mine, t, t).wait_send()
             f_copy(mine, t, t).wait_send()
             f_copy(t, t, t).wait_recv()
 
@@ -451,22 +562,6 @@
 def per_device(nd, nc, queries, key_rows, value_rows, attn_out, out_grad, log_sums, chosen, inputs):
     rows, heads, depth = queries.shape[1:]
     width = inputs.shape[2]
-    topk = chosen.shape[3]
-    me = lax.axis_index("ctx")
-
-    def by_head(array):
-        return jnp.swapaxes(array[0], 0, 1)
-
-    delta = jnp.sum(out_grad[0].astype(jnp.float32) * attn_out[0].astype(jnp.float32), -1).T
-    flat = chosen.reshape(heads * topk)
-    live = flat < me
-    order = jnp.arange(heads * topk, dtype=jnp.int32)
-    same = (flat[:, None] == flat[None, :]) & live[None, :] & (order[None, :] < order[:, None])
-    rank = jnp.sum(same.astype(jnp.int32), -1)
-    spot = jnp.where(live, CAP * flat + rank, CAP * nc)
-    hit = (spot[None, :] == jnp.arange(128, dtype=jnp.int32)[:, None]) & live[None, :]
-    ids = jnp.sum(jnp.where(hit, order[None, :] // topk, 0), -1)
-    alive = jnp.sum(hit.astype(jnp.int32), -1)
     slots = nc * CAP
     bf16, f32 = jnp.bfloat16, jnp.float32
     chips = nc // 2
@@ -479,14 +574,20 @@
     outs = pl.pallas_call(
         functools.partial(kernel, nd, nc),
         out_shape=(
-            jax.ShapeDtypeStruct((heads, rows, depth), bf16),
-            jax.ShapeDtypeStruct((heads, rows, depth), bf16),
-            jax.ShapeDtypeStruct((heads, rows, depth), bf16),
+            jax.ShapeDtypeStruct((rows, heads, depth), bf16),
+            jax.ShapeDtypeStruct((rows, heads, depth), bf16),
+            jax.ShapeDtypeStruct((rows, heads, depth), bf16),
             jax.ShapeDtypeStruct((8, heads * depth), f32),
         ),
-        in_specs=[vmem] * 8 + [smem] * 3,
+        in_specs=[vmem] * 7 + [smem],
         out_specs=(vmem,) * 4,
-        scratch_shapes=[
+        scratch_shapes=[pltpu.VMEM((heads, rows, depth), bf16)] * 7
+        + [
+            pltpu.VMEM((heads, rows), f32),
+            pltpu.VMEM((1, 128), jnp.int32),
+            pltpu.VMEM((1, 128), jnp.int32),
+            pltpu.SMEM((1, 128), jnp.int32),
+            pltpu.SMEM((1, 128), jnp.int32),
             pltpu.VMEM((nc, 1, 128), jnp.int32),
             pltpu.SMEM((nc, 1, 128), jnp.int32),
             pltpu.SMEM((heads,), jnp.int32),
@@ -501,11 +602,13 @@
             pltpu.VMEM((heads + slots, rows, depth), f32),
             pltpu.VMEM((2 * nd * rows, width), bf16),
             pltpu.VMEM((2 * nd * rows, depth), bf16),
+            pltpu.VMEM((nd, depth, span), f32),
             pltpu.VMEM((chips, nd, span // chips, depth), bf16),
             pltpu.VMEM((chips, nd, span // chips, depth), bf16),
             pltpu.VMEM((nd, span // chips, depth), f32),
             pltpu.VMEM((2 * nd, 8, depth), f32),
             dma(()),
+            dma((2,)),
             dma((nc,)),
             dma((nc,)),
             dma((nc,)),
@@ -522,8 +625,8 @@
             dma((nd,)),
             dma((2 * nd,)),
             dma((2 * nd,)),
-            dma((chips,)),
-            dma((chips,)),
+            dma((2, chips)),
+            dma((2, chips)),
             dma((2 * nd,)),
             dma((2 * nd,)),
         ],
@@ -531,25 +634,17 @@
             collective_id=0, has_side_effects=True, vmem_limit_bytes=58 * 1024 * 1024
         ),
     )(
-        by_head(queries),
-        by_head(key_rows),
-        by_head(value_rows),
-        by_head(out_grad),
+        queries[0],
+        key_rows[0],
+        value_rows[0],
+        attn_out[0],
+        out_grad[0],
         inputs[0],
         log_sums[0],
-        delta,
-        ids[None],
-        ids[:slots].reshape(nc, CAP),
-        alive[:slots].reshape(nc, CAP),
-        spot.reshape(heads, topk),
+        chosen[0, 0],
     )
     query_grad, key_grad, value_grad, weight_grad = outs
-    return (
-        jnp.swapaxes(query_grad, 0, 1)[None],
-        jnp.swapaxes(key_grad, 0, 1)[None],
-        jnp.swapaxes(value_grad, 0, 1)[None],
-        weight_grad,
-    )
+    return query_grad[None], key_grad[None], value_grad[None], weight_grad
 
 
 def solution(mesh):

time: 137 us -> 160 us (1.17)
  Pallas kernels: 123 us -> 153 us
  local copies, waits for them, and re-layouts: 10.2 us -> 6 us
  other arithmetic: 3.16 us -> 0 us
    pallas_call x1, Pallas kernels: 123 us -> 153 us  [per_device(): pl.pallas_call(functools.partial(kernel, nd, nc), out_shape=(jax.ShapeDty...]
    transpose x2 -> x0, local copies, waits for them, and re-layouts: 2.56 us -> none  [by_head(): return jnp.swapaxes(array[0], 0, 1)]
    reduce_sum x3 -> x0, other arithmetic: 2.51 us -> none  [the longest x1 2.23 us: per_device(): jnp.sum(out_grad[0].astype(jnp.float32) * attn_out[0].astype(jnp.float32)...]
    unnamed x23 -> x12, local copies, waits for them, and re-layouts: 5.92 us -> 5.32 us
where the time goes in v2:
time: 160 us; the launch traced here: 159 us
  Pallas kernels  153 us (96%)
  local copies, waits for them, and re-layouts  6 us (4%)
    pallas_call x1, Pallas kernels, per_device(): pl.pallas_call(functools.partial(kernel, nd, nc), out_shape=(jax.ShapeDty...  153 us
    unnamed x12, local copies, waits for them, and re-layouts  5.32 us

profile of v2, /device:TPU:1, one launch (start us, length us, event | category | flops | bytes accessed | tf_op | source)
XLA Modules:
  0.0 159.3 jit_solution(614245425510330591)
XLA Ops:
  0.6 0.0 copy-start.3
  0.6 0.7 copy-done.3
  1.3 0.7 copy.13
  2.0 152.7 %shard_map.111 = (bf16[128,16,128]{2,1,0:T(8,128)(2,1)}, bf16[128,16,128]{2,1,0:T(8,128)(2,1)}, bf16[128,16,128]{2,1,0:T(8,128)(2,1)}, f32[8,2048]{1,0:T(8,128)}) custom-call(bf16[128,16,128]{2,1,0:T(8,128)(2,1)} %bitcast.14, bf16[128,16,128]{2,1,0:T(8,128)(2,1)} %bitcast.15, bf16[128,16,128]{2,1,0:T(8,128)(2,1)} %bitcast.16, ...), custom_call_target="tpu_custom_call" | custom-call | tf_op jit(solution)/shard_map/pallas_call | solution.py:574
  154.7 0.0 copy-start.1
  154.7 1.9 %copy.18 = bf16[1,128,16,128]{3,2,1,0:T(8,128)(2,1)} copy(bf16[1,128,16,128]{3,2,1,0:T(8,128)(2,1)} %bitcast.13) | data formatting | bytes 1048576
  156.6 0.0 copy-done.1
  156.6 0.0 copy-start
  156.6 0.8 copy.19
  157.4 0.4 copy-done
  157.9 0.0 copy-start.2
  157.9 0.8 copy.20
  158.7 0.1 copy-done.2
  158.7 0.6 copy.21
Async XLA Ops:
  0.6 0.7 copy-start.3
  154.7 1.9 %copy-start.1 = (bf16[128,16,128]{2,1,0:T(8,128)(2,1)S(1)}, bf16[128,16,128]{2,1,0:T(8,128)(2,1)}, u32[]{:S(2)}) copy-start(bf16[128,16,128]{2,1,0:T(8,128)(2,1)} %get-tuple-element.9) | copy-start | bytes 1572868
  156.6 1.2 copy-start
  157.9 0.9 copy-start.2

commit v3 on v2

v3 whole, which is shorter than its diff:
```python
import functools

import jax
import jax.numpy as jnp
from jax import lax
from jax.experimental import pallas as pl
from jax.experimental.pallas import tpu as pltpu
from jax.sharding import PartitionSpec as P

CAP = 2
MESH = pl.DeviceIdType.MESH
DEAD = 1e30
AHEAD = 4
FIRST = 4
MARK = 4
STRIDE = 4
TURNS = 2
LSE_UNIT = 2.0**24
DELTA_UNIT = 2.0**18
NT = (((1,), (1,)), ((), ()))
NN = (((1,), (0,)), ((), ()))
TN = (((0,), (0,)), ((), ()))


def mm(a, b, dims):
    return lax.dot_general(a, b, dims, preferred_element_type=jnp.float32)


def pair_grads(query, grad, key, value, lse, delta, scale, keep=None):
    scores = mm(key, query, NT) * scale
    probs = jnp.exp(scores - lse)
    if keep is not None:
        probs = jnp.where(keep, probs, 0.0)
    dprobs = mm(value, grad, NT)
    dscores = (probs * (dprobs - delta)).astype(jnp.bfloat16)
    query_part = mm(dscores, key, TN) * scale
    key_part = mm(dscores, query, NN) * scale
    value_part = mm(probs.astype(jnp.bfloat16), grad, NN)
    return query_part, key_part, value_part


def kernel(
    nd,
    nc,
    q_in,
    k_in,
    v_in,
    o_in,
    g_in,
    x_ref,
    lse_ref,
    pick_ref,
    qg_out,
    dk_out,
    dv_out,
    wg_ref,
    q_ref,
    k_ref,
    v_ref,
    g_ref,
    qg_ref,
    dk_ref,
    dv_ref,
    delta_ref,
    lse_code,
    delta_own,
    ids_ref,
    pos_row,
    head_ref,
    pos_ref,
    ids_smem,
    last_smem,
    fwd_out,
    fwd_in,
    stat_out,
    stat_in,
    ret_out,
    ret_in,
    own_q,
    arena_k,
    arena_v,
    x_all,
    qg_all,
    w_acc,
    w_out,
    w_in,
    w_sum,
    w_fin,
    local_sem,
    table_sem,
    fwd_send,
    fwd_recv,
    stat_send,
    stat_recv,
    ret_send,
    ret_recv,
    up_send,
    up_recv,
    down_send,
    down_recv,
    sib_send,
    sib_recv,
    qg_send,
    qg_recv,
    hand_send,
    hand_recv,
    w_send,
    w_recv,
    f_send,
    f_recv,
):
    rows, heads, depth = q_in.shape
    topk = pick_ref.shape[1]
    scale = depth ** (-0.5)
    half_width = x_ref.shape[1] // 2
    share = nd // 2
    span = half_width // share
    me = lax.axis_index("ctx")
    zd = lax.axis_index("dp")
    core = lax.rem(me, 2)
    chip = me // 2
    chips = nc // 2

    def peer(j):
        return {"dp": zd, "ctx": j}

    barrier = pltpu.get_barrier_semaphore()

    def greet(where):
        pl.semaphore_signal(barrier, inc=1, device_id=where, device_id_type=MESH)

    for step in (1, nd - 1):
        greet({"dp": lax.rem(zd + step, nd), "ctx": me})

    @pl.when(core == 1)
    def _():
        greet(peer(me - 1))

    @pl.loop(1, nc)
    def _(n):
        i = nc - n

        @pl.when(i > me)
        def _():
            greet(peer(i))

    def x_rows(shard, which, count):
        return pl.ds(pl.multiple_of((2 * shard + which) * rows, rows), count * rows)

    def x_columns(which):
        return pl.ds(pl.multiple_of(which * half_width, half_width), half_width)

    seat = pltpu.make_async_copy(
        x_ref.at[:, x_columns(core)], x_all.at[x_rows(zd, core, 1)], local_sem
    )
    seat.start()

    lane = lax.broadcasted_iota(jnp.int32, (1, 128), 1)
    block = lax.shift_right_logical(lane, 1)
    slot = lane - 2 * block
    earlier = jnp.where(block < me, block, -1)
    ids = jnp.full((1, 128), heads, jnp.int32)
    count = jnp.zeros((1, 128), jnp.int32)
    picks = jnp.zeros((1, 128), jnp.int32)
    for e in range(heads * topk):
        target = pick_ref[e // topk, e % topk]
        hit = earlier == target
        ids = jnp.where(hit & (count == slot), e // topk, ids)
        count = count + hit.astype(jnp.int32)
        picks = jnp.where(lane == e, target, picks)
    ids_ref[...] = ids
    rank = jnp.zeros((1, 128), jnp.int32)
    for e in range(heads * topk):
        target = pick_ref[e // topk, e % topk]
        rank = rank + ((picks == target) & (lane > e)).astype(jnp.int32)
    pos_row[...] = jnp.where(picks < me, CAP * picks + rank, CAP * nc)
    tables = [
        pltpu.make_async_copy(ids_ref, head_ref, table_sem.at[0]),
        pltpu.make_async_copy(pos_row, pos_ref, table_sem.at[1]),
    ]
    for table in tables:
        table.start()

    q_ref[...] = jnp.swapaxes(q_in[...], 0, 1)
    g_ref[...] = jnp.swapaxes(g_in[...], 0, 1)
    delta = jnp.zeros((heads, rows), jnp.float32)
    for b in range(8):
        part = slice(b * rows // 8, (b + 1) * rows // 8)
        product = g_in[part].astype(jnp.float32) * o_in[part].astype(jnp.float32)
        sums = jnp.sum(product, -1, keepdims=True)
        shape = (rows // 8, heads, rows)
        token = lax.broadcasted_iota(jnp.int32, shape, 0) + b * rows // 8
        seat_of = lax.broadcasted_iota(jnp.int32, shape, 2)
        delta = delta + jnp.sum(jnp.where(token == seat_of, sums, 0.0), 0)
    delta_ref[...] = jnp.round(delta * DELTA_UNIT).astype(jnp.int32)
    lse_code[...] = jnp.round(lse_ref[...] * LSE_UNIT).astype(jnp.int32)
    delta_own[...] = delta

    for table in tables:
        table.wait()
    seat.wait()
    pl.semaphore_wait(barrier, me + 3 - core)

    lines = nc // 8

    def partner(n, sign):
        a = n % lines
        b = lax.rem(n // lines + 4 * lax.rem(a, 2), 8)
        line = lax.rem(me // 8 + sign * a + lines, lines)
        return 8 * line + lax.rem(lax.rem(me, 8) + sign * b + 8, 8)

    def fwd_copy(src, j, dst):
        return pltpu.make_async_remote_copy(
            src_ref=fwd_out.at[j],
            dst_ref=fwd_in.at[src],
            send_sem=fwd_send.at[j],
            recv_sem=fwd_recv.at[src],
            device_id=peer(dst),
            device_id_type=MESH,
        )

    def stat_copy(src, j, dst):
        return pltpu.make_async_remote_copy(
            src_ref=stat_out.at[j],
            dst_ref=stat_in.at[src],
            send_sem=stat_send.at[j],
            recv_sem=stat_recv.at[src],
            device_id=peer(dst),
            device_id_type=MESH,
        )

    def ret_copy(src, j, dst):
        return pltpu.make_async_remote_copy(
            src_ref=ret_out.at[j],
            dst_ref=ret_in.at[pl.ds(CAP * src, CAP)],
            send_sem=ret_send.at[j],
            recv_sem=ret_recv.at[src],
            device_id=peer(dst),
            device_id_type=MESH,
        )

    ups = nd // 2
    downs = nd - 1 - ups

    def ring_copy(shard, u, s, step, send_sem, recv_sem):
        piece = x_all.at[x_rows(shard, core if u == 0 else 1 - core, 1)]
        return pltpu.make_async_remote_copy(
            src_ref=piece,
            dst_ref=piece,
            send_sem=send_sem.at[s, u],
            recv_sem=recv_sem.at[s, u],
            device_id={"dp": lax.rem(zd + step, nd), "ctx": me},
            device_id_type=MESH,
        )

    def up_copy(shard, u, s):
        return ring_copy(shard, u, s, 1, up_send, up_recv)

    def down_copy(shard, u, s):
        return ring_copy(shard, u, s, nd - 1, down_send, down_recv)

    def sib_copy(which):
        return pltpu.make_async_remote_copy(
            src_ref=x_ref.at[:, x_columns(1 - core)],
            dst_ref=x_all.at[x_rows(zd, which, 1)],
            send_sem=sib_send.at[0],
            recv_sem=sib_recv.at[0],
            device_id=peer(2 * chip + 1 - core),
            device_id_type=MESH,
        )

    def below(s):
        return lax.rem(zd + nd - s, nd)

    def above(s):
        return lax.rem(zd + s, nd)

    def relay(k, u):
        if k == 0:
            if u == 1:
                sib_copy(1 - core).wait_recv()
            up_copy(zd, u, 0).start()
            if downs:
                down_copy(zd, u, 0).start()
            return
        up_copy(below(k), u, k - 1).wait_recv()
        if k < ups:
            up_copy(below(k), u, k).start()
        if k <= downs:
            down_copy(above(k), u, k - 1).wait_recv()
            if k < downs:
                down_copy(above(k), u, k).start()

    sib_copy(core).start()
    relay(0, 0)

    def send_pairs(n):
        j = partner(n, -1)

        @pl.when(j < me)
        def _():
            for s in range(CAP):
                code = head_ref[0, CAP * j + s]
                h = jnp.where(code < heads, code, 0)
                fwd_out[j, s, 0] = q_ref[h]
                fwd_out[j, s, 1] = g_ref[h]
            fwd_copy(me, j, j).start()

    @pl.loop(1, FIRST)
    def _(n):
        send_pairs(n)

    @pl.loop(1, nc)
    def _(n):
        j = partner(n, -1)

        @pl.when(j < me)
        def _():
            for s in range(CAP):
                code = head_ref[0, CAP * j + s]
                h = jnp.where(code < heads, code, 0)
                stat_out[j, pl.ds(s, 1), :] = lse_code[pl.ds(h, 1), :]
                stat_out[j, pl.ds(CAP + s, 1), :] = delta_ref[pl.ds(h, 1), :]
            stat_out[j, pl.ds(2 * CAP, 1), :] = ids_ref[...]
            stat_copy(me, j, j).start()

    relay(0, 1)

    @pl.loop(FIRST, min(AHEAD + 1, nc))
    def _(n):
        send_pairs(n)

    k_ref[...] = jnp.swapaxes(k_in[...], 0, 1)
    v_ref[...] = jnp.swapaxes(v_in[...], 0, 1)

    key_pos = lax.broadcasted_iota(jnp.int32, (rows, rows), 0)
    query_pos = lax.broadcasted_iota(jnp.int32, (rows, rows), 1)
    causal = key_pos <= query_pos

    @pl.loop(0, heads // 2)
    def _(n):
        for s in range(2):
            h = 2 * n + s
            query_part, key_part, value_part = pair_grads(
                q_ref[h],
                g_ref[h],
                k_ref[h],
                v_ref[h],
                lse_ref[pl.ds(h, 1), :],
                delta_own[pl.ds(h, 1), :],
                scale,
                causal,
            )
            own_q[h] = query_part
            arena_k[h] = key_part
            arena_v[h] = value_part

    for h in range(heads):
        last_smem[h] = h

    @pl.loop(me + 1, nc)
    def _(i):
        stat_copy(i, i, i).wait_recv()

    to_smem = pltpu.make_async_copy(stat_in.at[:, pl.ds(2 * CAP, 1)], ids_smem, local_sem)
    to_smem.start()
    to_smem.wait()

    @pl.loop(1, nc)
    def _(step):
        i = partner(step, 1)

        @pl.when(step + AHEAD < nc)
        def _():
            sent = partner(step, -1)

            @pl.when(sent < me)
            def _():
                fwd_copy(me, sent, sent).wait_send()

            send_pairs(step + AHEAD)

        @pl.when(i > me)
        def _():
            fwd_copy(i, i, i).wait_recv()
            for s in range(CAP):
                code = ids_smem[i, 0, CAP * me + s]
                alive = code < heads
                h = jnp.where(alive, code, 0)
                lse = stat_in[i, pl.ds(s, 1), :].astype(jnp.float32) * (1.0 / LSE_UNIT)
                row = heads + CAP * i + s
                query_part, key_part, value_part = pair_grads(
                    fwd_in[i, s, 0],
                    fwd_in[i, s, 1],
                    k_ref[h],
                    v_ref[h],
                    jnp.where(alive, lse, DEAD),
                    stat_in[i, pl.ds(CAP + s, 1), :].astype(jnp.float32) * (1.0 / DELTA_UNIT),
                    scale,
                )
                ret_out[i, s] = query_part.astype(jnp.bfloat16)
                before = last_smem[h]
                arena_k[row] = arena_k[before] + key_part
                arena_v[row] = arena_v[before] + value_part
                for t in range(heads):
                    last_smem[t] = jnp.where(h == t, row, last_smem[t])
            ret_copy(me, i, i).start()

        for event in range(2 * (ups - 1)):

            @pl.when(step == MARK + STRIDE * event)
            def _():
                relay(1 + event // 2, event % 2)

    ret_in[CAP * nc] = jnp.zeros((rows, depth), jnp.bfloat16)

    @pl.loop(0, me)
    def _(j):
        ret_copy(j, j, j).wait_recv()

    def qg_copy(src, shard):
        return pltpu.make_async_remote_copy(
            src_ref=qg_ref.at[pl.ds(2 * shard, 2)],
            dst_ref=qg_all.at[src, core],
            send_sem=qg_send.at[shard],
            recv_sem=qg_recv.at[src],
            device_id={"dp": shard, "ctx": me},
            device_id_type=MESH,
        )

    def hand_copy(shard, which):
        return pltpu.make_async_remote_copy(
            src_ref=qg_all.at[shard, which],
            dst_ref=qg_all.at[shard, which],
            send_sem=hand_send.at[shard],
            recv_sem=hand_recv.at[shard],
            device_id=peer(2 * chip + 1 - core),
            device_id_type=MESH,
        )

    offsets = [0]
    for k in range(1, nd // 2 + 1):
        offsets += [k] if 2 * k == nd else [k, nd - k]

    for offset in reversed(offsets):
        shard = above(offset)
        for which in range(2):
            h = 2 * shard + which
            total = own_q[h]
            for e in range(topk):
                total = total + ret_in[pos_ref[0, topk * h + e]].astype(jnp.float32)
            qg_ref[h] = total.astype(jnp.bfloat16)
        if offset:
            qg_copy(zd, shard).start()
        else:
            qg_all[zd, core] = qg_ref[pl.ds(2 * shard, 2)]
            hand_copy(zd, core).start()

    qg_out[...] = jnp.swapaxes(qg_ref[...], 0, 1)

    @pl.loop(0, heads)
    def _(h):
        at = last_smem[h]
        dk_ref[h] = arena_k[at].astype(jnp.bfloat16)
        dv_ref[h] = arena_v[at].astype(jnp.bfloat16)

    dk_out[...] = jnp.swapaxes(dk_ref[...], 0, 1)
    dv_out[...] = jnp.swapaxes(dv_ref[...], 0, 1)

    def add_chip(shard, r):
        flat = [jnp.concatenate([qg_all[shard, c, 0], qg_all[shard, c, 1]], 1) for c in range(2)]
        columns = pl.ds(pl.multiple_of(r * span, span), span)
        return mm(jnp.concatenate(flat, 0), x_all[x_rows(shard, 0, 2), columns], TN)

    turns = min(TURNS, share)
    turn_share = share // turns

    def w_copy(src, t, dst, turn):
        part = pl.ds(turn * turn_share, turn_share)
        return pltpu.make_async_remote_copy(
            src_ref=w_out.at[t, part],
            dst_ref=w_in.at[src, part],
            send_sem=w_send.at[turn, t],
            recv_sem=w_recv.at[turn, src],
            device_id=peer(2 * dst + core),
            device_id_type=MESH,
        )

    wide = chips // lines

    def chip_partner(n, sign):
        a = n % lines
        b = lax.rem(n // lines + (wide // 2) * lax.rem(a, 2), wide)
        line = lax.rem(chip // wide + sign * a + lines, lines)
        return wide * line + lax.rem(lax.rem(chip, wide) + sign * b + wide, wide)

    def hand_on(offset):
        shard = above(offset)
        qg_copy(shard, shard).wait_recv()
        hand_copy(shard, core).start()

    for place, offset in enumerate(offsets):
        shard = above(offset)
        if place + 1 < nd:
            hand_on(offsets[place + 1])
        hand_copy(shard, 1 - core).wait_recv()
        if place < nd - 1:

            @pl.loop(0, share)
            def _(r):
                part = add_chip(shard, r)
                w_acc[r] = part if place == 0 else w_acc[r] + part

            if place == 0:

                @pl.loop(0, nc)
                def _(j):
                    @pl.when(j < me)
                    def _():
                        stat_copy(me, j, j).wait_send()

                    @pl.when(j > me)
                    def _():
                        ret_copy(me, j, j).wait_send()

                @pl.loop(max(1, nc - AHEAD), nc)
                def _(n):
                    sent = partner(n, -1)

                    @pl.when(sent < me)
                    def _():
                        fwd_copy(me, sent, sent).wait_send()

                sib_copy(core).wait_send()
                for u in range(2):
                    relay(ups, u)
                    for s in range(ups):
                        up_copy(zd, u, s).wait_send()
                    for s in range(downs):
                        down_copy(zd, u, s).wait_send()
        else:
            for turn in range(turns):

                @pl.loop(turn * turn_share, (turn + 1) * turn_share)
                def _(r):
                    part = w_acc[r] + add_chip(shard, r)
                    w_out[:, r] = part.T.astype(jnp.bfloat16).reshape(chips, span // chips, 2 * depth)

                @pl.loop(1, chips)
                def _(n):
                    t = chip_partner(n, -1)
                    w_copy(chip, t, t, turn).start()

    for offset in offsets:
        if offset:
            qg_copy(zd, above(offset)).wait_send()
        hand_copy(above(offset), core).wait_send()

    def f_copy(src, q, which, shard):
        return pltpu.make_async_remote_copy(
            src_ref=w_sum.at[q, pl.ds(8 * which, 8)],
            dst_ref=w_fin.at[src],
            send_sem=f_send.at[q, which],
            recv_sem=f_recv.at[src],
            device_id={"dp": shard, "ctx": 2 * chip + which},
            device_id_type=MESH,
        )

    for turn in range(turns):
        part = pl.ds(turn * turn_share, turn_share)

        def add_part(n, total):
            t = chip_partner(n, 1)
            w_copy(t, t, t, turn).wait_recv()
            return total + w_in[t, part].astype(jnp.float32)

        w_sum[part] = lax.fori_loop(1, chips, add_part, w_out[chip, part].astype(jnp.float32))
        for q in range(turn * turn_share, (turn + 1) * turn_share):
            shard = share * core + q
            for which in range(2):
                at_home = (shard == zd) & (core == which)

                @pl.when(at_home)
                def _():
                    w_fin[zd] = w_sum[q, 8 * which : 8 * which + 8]

                @pl.when(jnp.logical_not(at_home))
                def _():
                    f_copy(zd, q, which, shard).start()

    @pl.loop(1, chips)
    def _(n):
        t = chip_partner(n, -1)
        for turn in range(turns):
            w_copy(chip, t, t, turn).wait_send()

    for q in range(share):
        shard = share * core + q
        for which in range(2):

            @pl.when((shard != zd) | (core != which))
            def _():
                f_copy(zd, q, which, shard).wait_send()

    for t in range(nd):

        @pl.when((zd != t) | (zd // share != core))
        def _():
            f_copy(t, 0, 0, 0).wait_recv()

        wg_ref[:, 2 * t * depth : 2 * (t + 1) * depth] = w_fin[t]


def per_device(nd, nc, queries, key_rows, value_rows, attn_out, out_grad, log_sums, chosen, inputs):
    rows, heads, depth = queries.shape[1:]
    width = inputs.shape[2]
    slots = nc * CAP
    bf16, f32 = jnp.bfloat16, jnp.float32
    chips = nc // 2
    share = nd // 2
    span = width // 2 // share
    vmem = pl.BlockSpec(memory_space=pltpu.VMEM)
    smem = pl.BlockSpec(memory_space=pltpu.SMEM)
    dma = pltpu.SemaphoreType.DMA
    ups = nd // 2
    downs = nd - 1 - ups
    outs = pl.pallas_call(
        functools.partial(kernel, nd, nc),
        out_shape=(
            jax.ShapeDtypeStruct((rows, heads, depth), bf16),
            jax.ShapeDtypeStruct((rows, heads, depth), bf16),
            jax.ShapeDtypeStruct((rows, heads, depth), bf16),
            jax.ShapeDtypeStruct((8, heads * depth), f32),
        ),
        in_specs=[vmem] * 7 + [smem],
        out_specs=(vmem,) * 4,
        scratch_shapes=[pltpu.VMEM((heads, rows, depth), bf16)] * 7
        + [
            pltpu.VMEM((heads, rows), jnp.int32),
            pltpu.VMEM((heads, rows), jnp.int32),
            pltpu.VMEM((heads, rows), f32),
            pltpu.VMEM((1, 128), jnp.int32),
            pltpu.VMEM((1, 128), jnp.int32),
            pltpu.SMEM((1, 128), jnp.int32),
            pltpu.SMEM((1, 128), jnp.int32),
            pltpu.SMEM((nc, 1, 128), jnp.int32),
            pltpu.SMEM((heads,), jnp.int32),
            pltpu.VMEM((nc, CAP, 2, rows, depth), bf16),
            pltpu.VMEM((nc, CAP, 2, rows, depth), bf16),
            pltpu.VMEM((nc, 8, 128), jnp.int32),
            pltpu.VMEM((nc, 8, 128), jnp.int32),
            pltpu.VMEM((nc, CAP, rows, depth), bf16),
            pltpu.VMEM((slots + 1, rows, depth), bf16),
            pltpu.VMEM((heads, rows, depth), f32),
            pltpu.VMEM((heads + slots, rows, depth), f32),
            pltpu.VMEM((heads + slots, rows, depth), f32),
            pltpu.VMEM((2 * nd * rows, width // 2), bf16),
            pltpu.VMEM((nd, 2, 2, rows, depth), bf16),
            pltpu.VMEM((share, 2 * depth, span), f32),
            pltpu.VMEM((chips, share, span // chips, 2 * depth), bf16),
            pltpu.VMEM((chips, share, span // chips, 2 * depth), bf16),
            pltpu.VMEM((share, span // chips, 2 * depth), f32),
            pltpu.VMEM((nd, 8, 2 * depth), f32),
            dma(()),
            dma((2,)),
            dma((nc,)),
            dma((nc,)),
            dma((nc,)),
            dma((nc,)),
            dma((nc,)),
            dma((nc,)),
            dma((ups, 2)),
            dma((ups, 2)),
            dma((max(downs, 1), 2)),
            dma((max(downs, 1), 2)),
            dma((1,)),
            dma((1,)),
            dma((nd,)),
            dma((nd,)),
            dma((nd,)),
            dma((nd,)),
            dma((2, chips)),
            dma((2, chips)),
            dma((share, 2)),
            dma((nd,)),
        ],
        compiler_params=pltpu.CompilerParams(
            collective_id=0, has_side_effects=True, vmem_limit_bytes=58 * 1024 * 1024
        ),
    )(
        queries[0],
        key_rows[0],
        value_rows[0],
        attn_out[0],
        out_grad[0],
        inputs[0],
        log_sums[0],
        chosen[0, 0],
    )
    query_grad, key_grad, value_grad, weight_grad = outs
    return query_grad[None], key_grad[None], value_grad[None], weight_grad


def solution(mesh):
    nd, nc = mesh.shape["dp"], mesh.shape["ctx"]
    four = P("dp", "ctx", None, None)
    return jax.shard_map(
        functools.partial(per_device, nd, nc),
        mesh=mesh,
        in_specs=(four, four, four, four, four, P("dp", None, "ctx"), four, P("dp", "ctx", None)),
        out_specs=(four, four, four, P(("dp", "ctx"), None)),
        check_vma=False,
    )
```

time: 160 us -> 121 us (0.76)
  Pallas kernels: 153 us -> 114 us
    pallas_call x1, Pallas kernels: 153 us -> 114 us  [per_device(): pl.pallas_call(functools.partial(kernel, nd, nc), out_shape=(jax.ShapeDty...]
where the time goes in v3:
time: 121 us; the launch traced here: 120 us
  Pallas kernels  114 us (94%)
  local copies, waits for them, and re-layouts  6 us (5%)
    pallas_call x1, Pallas kernels, per_device(): pl.pallas_call(functools.partial(kernel, nd, nc), out_shape=(jax.ShapeDty...  114 us
    unnamed x12, local copies, waits for them, and re-layouts  5.32 us

profile of v3, /device:TPU:1, one launch (start us, length us, event | category | flops | bytes accessed | tf_op | source)
XLA Modules:
  0.0 120.3 jit_solution(9117924624689609973)
XLA Ops:
  0.6 0.0 copy-start.3
  0.6 0.7 copy-done.3
  1.3 0.7 copy.13
  2.0 113.7 %shard_map.111 = (bf16[128,16,128]{2,1,0:T(8,128)(2,1)}, bf16[128,16,128]{2,1,0:T(8,128)(2,1)}, bf16[128,16,128]{2,1,0:T(8,128)(2,1)}, f32[8,2048]{1,0:T(8,128)}) custom-call(bf16[128,16,128]{2,1,0:T(8,128)(2,1)} %bitcast.14, bf16[128,16,128]{2,1,0:T(8,128)(2,1)} %bitcast.15, bf16[128,16,128]{2,1,0:T(8,128)(2,1)} %bitcast.16, ...), custom_call_target="tpu_custom_call" | custom-call | tf_op jit(solution)/shard_map/pallas_call | solution.py:627
  115.7 0.0 copy-start.1
  115.7 1.9 %copy.18 = bf16[1,128,16,128]{3,2,1,0:T(8,128)(2,1)} copy(bf16[1,128,16,128]{3,2,1,0:T(8,128)(2,1)} %bitcast.13) | data formatting | bytes 1048576
  117.6 0.0 copy-done.1
  117.6 0.0 copy-start
  117.6 0.8 copy.19
  118.4 0.4 copy-done
  118.8 0.0 copy-start.2
  118.8 0.8 copy.20
  119.6 0.1 copy-done.2
  119.7 0.6 copy.21
Async XLA Ops:
  0.6 0.7 copy-start.3
  115.7 1.9 %copy-start.1 = (bf16[128,16,128]{2,1,0:T(8,128)(2,1)S(1)}, bf16[128,16,128]{2,1,0:T(8,128)(2,1)}, u32[]{:S(2)}) copy-start(bf16[128,16,128]{2,1,0:T(8,128)(2,1)} %get-tuple-element.9) | copy-start | bytes 1572868
  117.6 1.2 %copy-start = (bf16[128,16,128]{2,1,0:T(8,128)(2,1)S(1)}, bf16[128,16,128]{2,1,0:T(8,128)(2,1)}, u32[]{:S(2)}) copy-start(bf16[128,16,128]{2,1,0:T(8,128)(2,1)} %get-tuple-element.10) | copy-start | bytes 1572868
  118.8 0.9 copy-start.2

commit v4 on v3

--- a/solution.py
+++ b/solution.py
@@ -10,10 +10,12 @@
 CAP = 2
 MESH = pl.DeviceIdType.MESH
 DEAD = 1e30
-AHEAD = 4
+LEAD = 4
+WINDOW = 4
+PLAIN = True
 FIRST = 4
-MARK = 4
-STRIDE = 4
+MARK = 2
+STRIDE = 3
 TURNS = 2
 LSE_UNIT = 2.0**24
 DELTA_UNIT = 2.0**18
@@ -81,6 +83,7 @@
     arena_v,
     x_all,
     qg_all,
+    qg_flip,
     w_acc,
     w_out,
     w_in,
@@ -169,35 +172,12 @@
         count = count + hit.astype(jnp.int32)
         picks = jnp.where(lane == e, target, picks)
     ids_ref[...] = ids
-    rank = jnp.zeros((1, 128), jnp.int32)
-    for e in range(heads * topk):
-        target = pick_ref[e // topk, e % topk]
-        rank = rank + ((picks == target) & (lane > e)).astype(jnp.int32)
-    pos_row[...] = jnp.where(picks < me, CAP * picks + rank, CAP * nc)
-    tables = [
-        pltpu.make_async_copy(ids_ref, head_ref, table_sem.at[0]),
-        pltpu.make_async_copy(pos_row, pos_ref, table_sem.at[1]),
-    ]
-    for table in tables:
-        table.start()
+    head_table = pltpu.make_async_copy(ids_ref, head_ref, table_sem.at[0])
+    head_table.start()
 
     q_ref[...] = jnp.swapaxes(q_in[...], 0, 1)
     g_ref[...] = jnp.swapaxes(g_in[...], 0, 1)
-    delta = jnp.zeros((heads, rows), jnp.float32)
-    for b in range(8):
-        part = slice(b * rows // 8, (b + 1) * rows // 8)
-        product = g_in[part].astype(jnp.float32) * o_in[part].astype(jnp.float32)
-        sums = jnp.sum(product, -1, keepdims=True)
-        shape = (rows // 8, heads, rows)
-        token = lax.broadcasted_iota(jnp.int32, shape, 0) + b * rows // 8
-        seat_of = lax.broadcasted_iota(jnp.int32, shape, 2)
-        delta = delta + jnp.sum(jnp.where(token == seat_of, sums, 0.0), 0)
-    delta_ref[...] = jnp.round(delta * DELTA_UNIT).astype(jnp.int32)
-    lse_code[...] = jnp.round(lse_ref[...] * LSE_UNIT).astype(jnp.int32)
-    delta_own[...] = delta
-
-    for table in tables:
-        table.wait()
+    head_table.wait()
     seat.wait()
     pl.semaphore_wait(barrier, me + 3 - core)
 
@@ -310,6 +290,27 @@
     def _(n):
         send_pairs(n)
 
+    delta = jnp.zeros((heads, rows), jnp.float32)
+    for b in range(8):
+        part = slice(b * rows // 8, (b + 1) * rows // 8)
+        product = g_in[part].astype(jnp.float32) * o_in[part].astype(jnp.float32)
+        sums = jnp.sum(product, -1, keepdims=True)
+        shape = (rows // 8, heads, rows)
+        token = lax.broadcasted_iota(jnp.int32, shape, 0) + b * rows // 8
+        seat_of = lax.broadcasted_iota(jnp.int32, shape, 2)
+        delta = delta + jnp.sum(jnp.where(token == seat_of, sums, 0.0), 0)
+    delta_ref[...] = jnp.round(delta * DELTA_UNIT).astype(jnp.int32)
+    lse_code[...] = jnp.round(lse_ref[...] * LSE_UNIT).astype(jnp.int32)
+    delta_own[...] = delta
+
+    rank = jnp.zeros((1, 128), jnp.int32)
+    for e in range(heads * topk):
+        target = pick_ref[e // topk, e % topk]
+        rank = rank + ((picks == target) & (lane > e)).astype(jnp.int32)
+    pos_row[...] = jnp.where(picks < me, CAP * picks + rank, CAP * nc)
+    pos_table = pltpu.make_async_copy(pos_row, pos_ref, table_sem.at[1])
+    pos_table.start()
+
     @pl.loop(1, nc)
     def _(n):
         j = partner(n, -1)
@@ -326,9 +327,20 @@
 
     relay(0, 1)
 
-    @pl.loop(FIRST, min(AHEAD + 1, nc))
+    def paced_send(n):
+        @pl.when(n > WINDOW)
+        def _():
+            sent = partner(n - WINDOW, -1)
+
+            @pl.when(sent < me)
+            def _():
+                fwd_copy(me, sent, sent).wait_send()
+
+        send_pairs(n)
+
+    @pl.loop(FIRST, min(LEAD + 1, nc))
     def _(n):
-        send_pairs(n)
+        paced_send(n)
 
     k_ref[...] = jnp.swapaxes(k_in[...], 0, 1)
     v_ref[...] = jnp.swapaxes(v_in[...], 0, 1)
@@ -370,15 +382,9 @@
     def _(step):
         i = partner(step, 1)
 
-        @pl.when(step + AHEAD < nc)
+        @pl.when(step + LEAD < nc)
         def _():
-            sent = partner(step, -1)
-
-            @pl.when(sent < me)
-            def _():
-                fwd_copy(me, sent, sent).wait_send()
-
-            send_pairs(step + AHEAD)
+            paced_send(step + LEAD)
 
         @pl.when(i > me)
         def _():
@@ -412,6 +418,8 @@
             def _():
                 relay(1 + event // 2, event % 2)
 
+    pos_table.wait()
+
     ret_in[CAP * nc] = jnp.zeros((rows, depth), jnp.bfloat16)
 
     @pl.loop(0, me)
@@ -467,10 +475,13 @@
     dk_out[...] = jnp.swapaxes(dk_ref[...], 0, 1)
     dv_out[...] = jnp.swapaxes(dv_ref[...], 0, 1)
 
-    def add_chip(shard, r):
+    def chip_columns(shard):
         flat = [jnp.concatenate([qg_all[shard, c, 0], qg_all[shard, c, 1]], 1) for c in range(2)]
+        return jnp.concatenate(flat, 0).T
+
+    def add_chip(flipped, shard, r):
         columns = pl.ds(pl.multiple_of(r * span, span), span)
-        return mm(jnp.concatenate(flat, 0), x_all[x_rows(shard, 0, 2), columns], TN)
+        return mm(flipped, x_all[x_rows(shard, 0, 2), columns], NN)
 
     turns = min(TURNS, share)
     turn_share = share // turns
@@ -504,11 +515,12 @@
         if place + 1 < nd:
             hand_on(offsets[place + 1])
         hand_copy(shard, 1 - core).wait_recv()
+        qg_flip[...] = chip_columns(shard)
         if place < nd - 1:
 
             @pl.loop(0, share)
             def _(r):
-                part = add_chip(shard, r)
+                part = add_chip(qg_flip[...], shard, r)
                 w_acc[r] = part if place == 0 else w_acc[r] + part
 
             if place == 0:
@@ -523,7 +535,7 @@
                     def _():
                         ret_copy(me, j, j).wait_send()
 
-                @pl.loop(max(1, nc - AHEAD), nc)
+                @pl.loop(max(1, nc - WINDOW), nc)
                 def _(n):
                     sent = partner(n, -1)
 
@@ -543,7 +555,7 @@
 
                 @pl.loop(turn * turn_share, (turn + 1) * turn_share)
                 def _(r):
-                    part = w_acc[r] + add_chip(shard, r)
+                    part = w_acc[r] + add_chip(qg_flip[...], shard, r)
                     w_out[:, r] = part.T.astype(jnp.bfloat16).reshape(chips, span // chips, 2 * depth)
 
                 @pl.loop(1, chips)
@@ -609,6 +621,12 @@
             f_copy(t, 0, 0, 0).wait_recv()
 
         wg_ref[:, 2 * t * depth : 2 * (t + 1) * depth] = w_fin[t]
+
+
+def hand_over(*refs):
+    count = len(refs) // 2
+    for source, target in zip(refs[:count], refs[count:]):
+        target[...] = source[...]
 
 
 def per_device(nd, nc, queries, key_rows, value_rows, attn_out, out_grad, log_sums, chosen, inputs):
@@ -656,6 +674,7 @@
             pltpu.VMEM((heads + slots, rows, depth), f32),
             pltpu.VMEM((2 * nd * rows, width // 2), bf16),
             pltpu.VMEM((nd, 2, 2, rows, depth), bf16),
+            pltpu.VMEM((2 * depth, 2 * rows), bf16),
             pltpu.VMEM((share, 2 * depth, span), f32),
             pltpu.VMEM((chips, share, span // chips, 2 * depth), bf16),
             pltpu.VMEM((chips, share, span // chips, 2 * depth), bf16),
@@ -697,6 +716,13 @@
         log_sums[0],
         chosen[0, 0],
     )
+    if PLAIN:
+        outs = pl.pallas_call(
+            hand_over,
+            out_shape=[jax.ShapeDtypeStruct(out.shape, out.dtype) for out in outs],
+            in_specs=[vmem] * 4,
+            out_specs=[vmem] * 4,
+        )(*outs)
     query_grad, key_grad, value_grad, weight_grad = outs
     return query_grad[None], key_grad[None], value_grad[None], weight_grad
 

time: 121 us -> 116 us (0.959)
  local copies, waits for them, and re-layouts: 6 us -> 1.35 us
    unnamed x12 -> x2, local copies, waits for them, and re-layouts: 5.32 us -> 0.67 us
    pallas_call x0 -> x1, Pallas kernels: none -> 2.54 us  [per_device(): pl.pallas_call(hand_over, out_shape=[jax.ShapeDtypeStruct(out.shape, out....]
    pallas_call x1, Pallas kernels: 114 us -> 112 us  [per_device(): pl.pallas_call(functools.partial(kernel, nd, nc), out_shape=(jax.ShapeDty...]
where the time goes in v4:
time: 116 us
  Pallas kernels  114 us (98%)
  local copies, waits for them, and re-layouts  1.35 us (1%)
    pallas_call x1, Pallas kernels, per_device(): pl.pallas_call(functools.partial(kernel, nd, nc), out_shape=(jax.ShapeDty...  112 us
    pallas_call x1, Pallas kernels, per_device(): pl.pallas_call(hand_over, out_shape=[jax.ShapeDtypeStruct(out.shape, out....  2.54 us

profile of v4, /device:TPU:1, one launch (start us, length us, event | category | flops | bytes accessed | tf_op | source)
XLA Modules:
  0.0 116.1 jit_solution(17525501654791419728)
XLA Ops:
  0.6 0.0 copy-start
  0.6 0.7 copy-done
  1.3 0.7 copy.13
  2.0 111.5 %shard_map.111 = (bf16[128,16,128]{2,1,0:T(8,128)(2,1)}, bf16[128,16,128]{2,1,0:T(8,128)(2,1)}, bf16[128,16,128]{2,1,0:T(8,128)(2,1)}, f32[8,2048]{1,0:T(8,128)}) custom-call(bf16[128,16,128]{2,1,0:T(8,128)(2,1)} %bitcast.11, bf16[128,16,128]{2,1,0:T(8,128)(2,1)} %bitcast.12, bf16[128,16,128]{2,1,0:T(8,128)(2,1)} %bitcast.13, ...), custom_call_target="tpu_custom_call" | custom-call | tf_op jit(solution)/shard_map/pallas_call | solution.py:645
  113.5 2.5 %shard_map.112 = (bf16[128,16,128]{2,1,0:T(8,128)(2,1)}, bf16[128,16,128]{2,1,0:T(8,128)(2,1)}, bf16[128,16,128]{2,1,0:T(8,128)(2,1)}, f32[8,2048]{1,0:T(8,128)}) custom-call(bf16[128,16,128]{2,1,0:T(8,128)(2,1)} %get-tuple-element.12.refs_0_, bf16[128,16,128]{2,1,0:T(8,128)(2,1)} %get-tuple-element.13.refs_1_, ...), custom_call_target="tpu_custom_call" | custom-call | tf_op jit(solution)/shard_map/pallas_call | solution.py:720
Async XLA Ops:
  0.6 0.7 copy-start

commit v5 on v4

--- a/solution.py
+++ b/solution.py
@@ -113,7 +113,7 @@
     f_recv,
 ):
     rows, heads, depth = q_in.shape
-    topk = pick_ref.shape[1]
+    topk = pick_ref.shape[0]
     scale = depth ** (-0.5)
     half_width = x_ref.shape[1] // 2
     share = nd // 2
@@ -166,7 +166,7 @@
     count = jnp.zeros((1, 128), jnp.int32)
     picks = jnp.zeros((1, 128), jnp.int32)
     for e in range(heads * topk):
-        target = pick_ref[e // topk, e % topk]
+        target = pick_ref[e % topk, 0, e // topk]
         hit = earlier == target
         ids = jnp.where(hit & (count == slot), e // topk, ids)
         count = count + hit.astype(jnp.int32)
@@ -305,7 +305,7 @@
 
     rank = jnp.zeros((1, 128), jnp.int32)
     for e in range(heads * topk):
-        target = pick_ref[e // topk, e % topk]
+        target = pick_ref[e % topk, 0, e // topk]
         rank = rank + ((picks == target) & (lane > e)).astype(jnp.int32)
     pos_row[...] = jnp.where(picks < me, CAP * picks + rank, CAP * nc)
     pos_table = pltpu.make_async_copy(pos_row, pos_ref, table_sem.at[1])
@@ -714,7 +714,7 @@
         out_grad[0],
         inputs[0],
         log_sums[0],
-        chosen[0, 0],
+        jnp.transpose(chosen[0], (2, 0, 1)),
     )
     if PLAIN:
         outs = pl.pallas_call(

time: 116 us -> 115 us (level)
  local copies, waits for them, and re-layouts: 1.35 us -> 0 us
where the time goes in v5:
time: 115 us
  Pallas kernels  114 us (99%)
    pallas_call x1, Pallas kernels, per_device(): pl.pallas_call(functools.partial(kernel, nd, nc), out_shape=(jax.ShapeDty...  112 us
    pallas_call x1, Pallas kernels, per_device(): pl.pallas_call(hand_over, out_shape=[jax.ShapeDtypeStruct(out.shape, out....  2.54 us

profile of v5, /device:TPU:1, one launch (start us, length us, event | category | flops | bytes accessed | tf_op | source)
XLA Modules:
  0.0 114.8 jit_solution(8971917720518429571)
XLA Ops:
  0.6 111.6 %shard_map.111 = (bf16[128,16,128]{2,1,0:T(8,128)(2,1)}, bf16[128,16,128]{2,1,0:T(8,128)(2,1)}, bf16[128,16,128]{2,1,0:T(8,128)(2,1)}, f32[8,2048]{1,0:T(8,128)}) custom-call(bf16[128,16,128]{2,1,0:T(8,128)(2,1)} %bitcast.13, bf16[128,16,128]{2,1,0:T(8,128)(2,1)} %bitcast.14, bf16[128,16,128]{2,1,0:T(8,128)(2,1)} %bitcast.15, ...), custom_call_target="tpu_custom_call" | custom-call | tf_op jit(solution)/shard_map/pallas_call | solution.py:645
  112.2 2.5 %shard_map.112 = (bf16[128,16,128]{2,1,0:T(8,128)(2,1)}, bf16[128,16,128]{2,1,0:T(8,128)(2,1)}, bf16[128,16,128]{2,1,0:T(8,128)(2,1)}, f32[8,2048]{1,0:T(8,128)}) custom-call(bf16[128,16,128]{2,1,0:T(8,128)(2,1)} %get-tuple-element.12.refs_0_, bf16[128,16,128]{2,1,0:T(8,128)(2,1)} %get-tuple-element.13.refs_1_, ...), custom_call_target="tpu_custom_call" | custom-call | tf_op jit(solution)/shard_map/pallas_call | solution.py:720
